TPU v7x, 256 devices: a whole 4x4x8 slice. The times are simulated.
256 devices in a mesh: space: 128 (over y, x, z), chan: 2 (over core).
Axes of the slice: x: 4, y: 4, z: 8, core: 2. Of those that a mesh axis runs over, the one named last changes fastest.
Arguments:
- features: bfloat16 [32, 4096, 512], P('chan', 'space'), may hold values from -6 to 6
- neighbours: int32 [4096, 6], P('space'), may hold values from -1 to 4095, as said below
- octants: int32 [4096], P('space'), may hold values from 0 to 7, as said below
- owners: int32 [512, 1], P('space'), may hold values from 0 to 15; in each aligned block of 4 rows (0 to 3, 4 to 7, ...) at most 2 rows name the same one
- coarse_field: bfloat16 [32, 4096, 512], P('chan', 'space'), may hold values from -6 to 6
- enc_weight: bfloat16 [7, 32, 32], replicated, may hold values from -0.375 to 0.375
- enc_bias: float32 [32], replicated, may hold values from -3 to 3
- coarse_weight: bfloat16 [7, 32, 32], replicated, may hold values from -0.375 to 0.375
- coarse_bias: float32 [32], replicated, may hold values from -3 to 3
- dec_weight: bfloat16 [7, 32, 32], replicated, may hold values from -0.375 to 0.375
- dec_bias: float32 [32], replicated, may hold values from -3 to 3
- psi_weight: bfloat16 [32, 3], replicated, may hold values from -1 to 1
Outputs:
- velocity: float32 [3, 4096, 512], P(None, 'space')
Inputs may be any that keep to these rules, and one draw needn't show every extreme that they name: `neighbours`: an entry that is not -1 names a block of the same device, or, for one of the first 8 blocks of a device and an even direction, one of the last 8 blocks of the device before, or, for one of the last 8 blocks and an odd direction, one of the first 8 blocks of the device after. `octants`: within each run of blocks 8 K to 8 K + 7 every octant appears once. `owners`: among the 4 coarse blocks of one device at most 2 have the same owner.
All inputs are finite; a program needn't handle non-finite values.
Results may differ from a plain program's by a relative error of at most 0.01.
Values may be sent and summed in bfloat16 or wider, within the bound.
A program may use at most 128 MiB of HBM per device.

v0:
```python
import math

import jax
import jax.numpy as jnp
import numpy as np
from jax import lax
from jax.sharding import PartitionSpec as P

WINDOW = 16
REACH = 8


def shifted(value, axis, steps):
    count = lax.axis_size(axis)
    first, last = (max(0, -steps), min(count, count - steps))
    return lax.ppermute(value, axis, [(source, source + steps) for source in range(first, last)])


def swapped(shard, axis, stride):
    return lax.ppermute(shard, axis, [(i, i ^ 1 << stride) for i in range(lax.axis_size(axis))])


def as_sent(shard):
    return jax.tree.map(lambda a: a.astype(jnp.bfloat16) if a.dtype == jnp.float32 else a, shard)


def voxel_tables():
    voxels = np.arange(512)
    coords = [voxels // 64, voxels // 8 % 8, voxels % 8]
    strides = [64, 8, 1]
    facepos = [
        (coords[1] * 8 + coords[2]).astype(np.int32),
        (coords[0] * 8 + coords[2]).astype(np.int32),
        (coords[0] * 8 + coords[1]).astype(np.int32),
    ]
    pieces = []
    for which_axis in range(3):
        for side_value in (0, 7):
            chosen = voxels[coords[which_axis] == side_value]
            pieces.append(chosen[np.argsort(facepos[which_axis][chosen])])
    face_index = np.concatenate(pieces).astype(np.int32)
    octant_voxel = coords[0] // 2 * 16 + coords[1] // 2 * 4 + coords[2] // 2
    pool_matrix = (octant_voxel[:, None] == np.arange(64)[None, :]).astype(np.float32) * 0.125
    octant_id = coords[0] // 4 * 4 + coords[1] // 4 * 2 + coords[2] // 4
    inner_voxel = coords[0] % 4 * 16 + coords[1] % 4 * 4 + coords[2] % 4
    to_coarse = (octant_id * 64 + inner_voxel).astype(np.int32)
    to_octants = np.argsort(to_coarse).astype(np.int32)
    return (coords, strides, facepos, face_index, pool_matrix, to_coarse, to_octants)


def make_taps(block_x, near_faces, tables):
    coords, strides, facepos = (tables[0], tables[1], tables[2])
    stencil = [block_x]
    for direction in range(6):
        which_axis = direction // 2
        step_sign = 1 if direction % 2 else -1
        rolled = jnp.roll(block_x, -step_sign * strides[which_axis], axis=2)
        on_edge = coords[which_axis] == (7 if step_sign > 0 else 0)
        face_fill = jnp.take(near_faces[direction], facepos[which_axis], axis=2)
        stencil.append(jnp.where(on_edge, face_fill, rolled))
    return jnp.stack(stencil)


def neighbour_faces(face_pool, index_rows):
    near_faces = []
    for direction in range(6):
        column = index_rows[:, direction]
        present = column >= 0
        opposite = direction ^ 1
        picked = jnp.take(
            face_pool[:, :, opposite * 64 : (opposite + 1) * 64],
            jnp.where(present, column, 0),
            axis=1,
        )
        near_faces.append(jnp.where(present[None, :, None], picked, jnp.zeros((), picked.dtype)))
    return near_faces


def derivative(stencil, axis_id, component):
    return (
        stencil[2 + 2 * axis_id, component].astype(jnp.float32)
        - stencil[1 + 2 * axis_id, component].astype(jnp.float32)
    ) * 0.5


def curl_field(stencil):
    return jnp.stack(
        [
            derivative(stencil, 1, 2) - derivative(stencil, 2, 1),
            derivative(stencil, 2, 0) - derivative(stencil, 0, 2),
            derivative(stencil, 0, 1) - derivative(stencil, 1, 0),
        ]
    )


def remote_faces(own_faces):
    row_count = own_faces.shape[1]
    lower_faces = shifted(own_faces[:, row_count - REACH :], "space", 1)
    upper_faces = shifted(own_faces[:, :REACH], "space", -1)
    return (lower_faces, upper_faces)


def window_route(pieces, mover):
    width = pieces.shape[0]
    member = lax.axis_index("space") % width
    order = jnp.bitwise_xor(member, jnp.arange(width, dtype=jnp.int32))
    held = jnp.take(pieces, order, axis=0)
    for bit in range(width.bit_length() - 1):
        split = held.reshape((width >> bit + 1, 2, 1 << bit) + held.shape[1:])
        moved = mover(split[:, 1], bit)
        held = jnp.stack([split[:, 0], moved], axis=1).reshape(held.shape)
    return jnp.take(held, order, axis=0)


def group_conv(full_input, face_pool, pool_index, weights, biases, out_low, out_count, tables):
    w_local = lax.dynamic_slice_in_dim(weights, out_low, out_count, 2)
    b_local = lax.dynamic_slice_in_dim(biases, out_low, out_count, 0)
    channels = full_input.shape[0]
    row_count = full_input.shape[1]
    group_size = math.gcd(32, row_count)

    def one_group(first_row):
        block_x = lax.dynamic_slice_in_dim(full_input, first_row, group_size, 1)
        if face_pool is None:
            near_faces = [jnp.zeros((channels, group_size, 64), jnp.bfloat16)] * 6
        else:
            index_rows = lax.dynamic_slice_in_dim(pool_index, first_row, group_size, 0)
            near_faces = neighbour_faces(face_pool, index_rows)
        stencil = make_taps(block_x, near_faces, tables)
        summed = (
            jnp.einsum("tcgv,tco->ogv", stencil, w_local, preferred_element_type=jnp.float32)
            + b_local[:, None, None]
        )
        return jax.nn.silu(summed).astype(jnp.bfloat16)

    first_rows = jnp.arange(row_count // group_size, dtype=jnp.int32) * group_size
    stacked = lax.map(one_group, first_rows)
    return stacked.transpose(1, 0, 2, 3).reshape(out_count, row_count, 512)


def fine_conv(xlocal, pool_index, weights, biases, out_low, tables):
    face_index = tables[3]
    own_faces = jnp.take(xlocal, face_index, axis=2)
    lower_faces, upper_faces = remote_faces(own_faces)
    full_input, lower_faces, upper_faces = (
        lax.all_gather(xlocal, "chan", axis=0, tiled=True),
        lax.all_gather(lower_faces, "chan", axis=0, tiled=True),
        lax.all_gather(upper_faces, "chan", axis=0, tiled=True),
    )
    face_pool = jnp.concatenate(
        [lower_faces, jnp.take(full_input, face_index, axis=2), upper_faces], axis=1
    )
    return group_conv(
        full_input, face_pool, pool_index, weights, biases, out_low, xlocal.shape[0], tables
    )


def on_device(
    features,
    neighbours,
    octants,
    owners,
    coarse_field,
    enc_weight,
    enc_bias,
    coarse_weight,
    coarse_bias,
    dec_weight,
    dec_bias,
    psi_weight,
):
    tables = voxel_tables()
    face_index, pool_matrix, to_coarse, to_octants = (tables[3], tables[4], tables[5], tables[6])
    local_ch = features.shape[0]
    blocks = features.shape[1]
    coarse_count = blocks // 8
    out_low = lax.axis_index("chan") * local_ch
    device = lax.axis_index("space")
    slot_count = coarse_field.shape[1]
    pair_slots = slot_count // WINDOW
    present = neighbours >= 0
    pool_index = jnp.where(present, neighbours - device * blocks + REACH, -1)
    encoded = fine_conv(features, pool_index, enc_weight, enc_bias, out_low, tables)
    pooled = jnp.einsum(
        "cbv,vq->cbq",
        encoded,
        jnp.asarray(pool_matrix, jnp.bfloat16),
        preferred_element_type=jnp.float32,
    ).astype(jnp.bfloat16)
    owner_local = owners[:, 0]
    positions = jnp.arange(coarse_count, dtype=jnp.int32)
    same_owner = owner_local[:, None] == owner_local[None, :]
    earlier = positions[None, :] < positions[:, None]
    slot_rank = jnp.sum((same_owner & earlier).astype(jnp.int32), axis=1)
    send_row = jnp.repeat(owner_local * pair_slots + slot_rank, 8) * 8 + octants
    octant_rows = pooled.transpose(1, 0, 2).reshape(blocks, local_ch * 64)
    outgoing = (
        jnp.zeros((slot_count * 8, local_ch * 64), jnp.bfloat16).at[send_row].set(octant_rows)
    )
    arrived = window_route(
        outgoing.reshape(WINDOW, pair_slots * 8, local_ch * 64),
        lambda part, bit: swapped(part, "space", bit),
    )
    arranged = (
        arrived.reshape(slot_count, 8, local_ch, 64)
        .transpose(2, 0, 1, 3)
        .reshape(local_ch, slot_count, 512)
    )
    arranged = jnp.take(arranged, to_coarse, axis=2)
    coarse_in = (arranged.astype(jnp.float32) + coarse_field.astype(jnp.float32)).astype(
        jnp.bfloat16
    )
    coarse_full = lax.all_gather(coarse_in, "chan", axis=0, tiled=True)
    coarse_out = group_conv(
        coarse_full, None, None, coarse_weight, coarse_bias, out_low, local_ch, tables
    )
    octant_order = jnp.take(coarse_out, to_octants, axis=2)
    returning = (
        octant_order.reshape(local_ch, slot_count, 8, 64)
        .transpose(1, 2, 0, 3)
        .reshape(WINDOW, pair_slots * 8, local_ch * 64)
    )
    returned = window_route(
        returning, lambda part, bit: swapped(as_sent(part), "space", bit).astype(part.dtype)
    )
    picked_rows = jnp.take(returned.reshape(slot_count * 8, local_ch * 64), send_row, axis=0)
    returned_octants = picked_rows.reshape(blocks, local_ch, 64).transpose(1, 0, 2)
    upsampled = jnp.einsum(
        "cbq,vq->cbv",
        returned_octants,
        jnp.asarray(pool_matrix * 8.0, jnp.bfloat16),
        preferred_element_type=jnp.float32,
    )
    decoder_in = (encoded.astype(jnp.float32) + upsampled).astype(jnp.bfloat16)
    decoded = fine_conv(decoder_in, pool_index, dec_weight, dec_bias, out_low, tables)
    psi_rows = lax.dynamic_slice_in_dim(psi_weight, out_low, local_ch, 0)
    partial_stream = jnp.einsum(
        "cbv,cm->mbv", decoded, psi_rows, preferred_element_type=jnp.float32
    )
    stream = lax.psum(partial_stream, "chan").astype(jnp.bfloat16)
    stream_faces = jnp.take(stream, face_index, axis=2)
    lower_faces, upper_faces = remote_faces(stream_faces)
    face_pool = jnp.concatenate([lower_faces, stream_faces, upper_faces], axis=1)
    stencil = make_taps(stream, neighbour_faces(face_pool, pool_index), tables)
    return curl_field(stencil)


def solution(mesh):
    return jax.shard_map(
        on_device,
        mesh=mesh,
        in_specs=(
            P("chan", "space", None),
            P("space", None),
            P("space"),
            P("space", None),
            P("chan", "space", None),
            P(),
            P(),
            P(),
            P(),
            P(),
            P(),
            P(),
        ),
        out_specs=P(None, "space", None),
        check_vma=False,
    )
```

profile of v0, /device:TPU:25, one launch (start us, length us, event | category | flops | bytes accessed | tf_op | source)
XLA Modules:
  0.0 508.8 jit_solution(17503255180518984238)
XLA Ops:
  23.6 8.2 %collective-permute-start.1 = (bf16[16,8,384]{2,1,0:T(8,128)(2,1)S(1)}, bf16[16,8,384]{2,1,0:T(8,128)(2,1)}, u32[]{:S(2)}, u32[]{:S(2)}) collective-permute-start(bf16[16,8,384]{2,1,0:T(8,128)(2,1)S(1)} %copy.587), channel_id=1, source_target_pairs={{2,0},{4,2},{6,4},{8,6},{10,8},{12,10},{14,12},{16,14},{18,16},{20... | collective-permute-start | bytes 294920 | tf_op jit(solution)/shard_map/ppermute | solution.py:16
  51.8 8.6 %copy.586 = bf16[32,32,512]{1,0,2:T(8,128)(2,1)} copy(bf16[32,32,512]{2,0,1:T(8,128)(2,1)} %all-gather.4.cloned.1.call-done) | data formatting | bytes 2097152 | tf_op jit(solution)/shard_map/all_gather | solution.py:146
  92.0 6.3 %copy.595 = bf16[512,32,32]{0,1,2:T(8,128)(2,1)} copy(bf16[512,32,32]{2,1,0:T(8,128)(2,1)} %gather_fusion.7) | data formatting | bytes 2097152 | tf_op jit(solution)/shard_map/while/body/eval_jaxpr/jit(_take)/gather | solution.py:59
  118.6 6.0 %copy.601 = bf16[512,32,32]{0,1,2:T(8,128)(2,1)} copy(bf16[512,32,32]{2,1,0:T(8,128)(2,1)} %gather_fusion.11) | data formatting | bytes 2097152 | tf_op jit(solution)/shard_map/while/body/eval_jaxpr/jit(_take)/gather | solution.py:59
  130.9 6.0 %copy.604 = bf16[512,32,32]{0,1,2:T(8,128)(2,1)} copy(bf16[512,32,32]{2,1,0:T(8,128)(2,1)} %gather_fusion.13) | data formatting | bytes 2097152 | tf_op jit(solution)/shard_map/while/body/eval_jaxpr/jit(_take)/gather | solution.py:59
  143.6 6.0 %copy.607 = bf16[512,32,32]{0,1,2:T(8,128)(2,1)} copy(bf16[512,32,32]{2,1,0:T(8,128)(2,1)} %gather_fusion.15) | data formatting | bytes 2097152 | tf_op jit(solution)/shard_map/while/body/eval_jaxpr/jit(_take)/gather | solution.py:59
  160.6 7.5 %collective-permute-done.2 = bf16[8,1,16,1024]{3,2,0,1:T(8,128)(2,1)S(1)} collective-permute-done((bf16[8,1,16,1024]{3,2,0,1:T(8,128)(2,1)S(1)}, bf16[8,1,16,1024]{3,2,0,1:T(8,128)(2,1)S(1)}, u32[]{:S(2)}, u32[]{:S(2)}) %collective-permute-start.2) | collective-permute-done | bytes 262176 | tf_op jit(solution)/shard_map/ppermute | solution.py:20
  168.2 14.7 %collective-permute-done.3 = bf16[4,2,16,1024]{3,2,0,1:T(8,128)(2,1)S(1)} collective-permute-done((bf16[4,2,16,1024]{3,2,0,1:T(8,128)(2,1)S(1)}, bf16[4,2,16,1024]{3,2,0,1:T(8,128)(2,1)S(1)}, u32[]{:S(2)}, u32[]{:S(2)}) %collective-permute-start.3) | collective-permute-done | bytes 262176 | tf_op jit(solution)/shard_map/ppermute | solution.py:20
  185.0 14.7 %collective-permute-done.4 = bf16[2,4,16,1024]{3,2,0,1:T(8,128)(2,1)S(1)} collective-permute-done((bf16[2,4,16,1024]{3,2,0,1:T(8,128)(2,1)S(1)}, bf16[2,4,16,1024]{3,2,0,1:T(8,128)(2,1)S(1)}, u32[]{:S(2)}, u32[]{:S(2)}) %collective-permute-start.4) | collective-permute-done | bytes 262176 | tf_op jit(solution)/shard_map/ppermute | solution.py:20
  199.9 7.4 %collective-permute-done.5 = bf16[1,8,16,1024]{3,2,1,0:T(8,128)(2,1)S(1)} collective-permute-done((bf16[1,8,16,1024]{3,2,1,0:T(8,128)(2,1)S(1)}, bf16[1,8,16,1024]{3,2,1,0:T(8,128)(2,1)S(1)}, u32[]{:S(2)}, u32[]{:S(2)}) %collective-permute-start.5) | collective-permute-done | bytes 262176 | tf_op jit(solution)/shard_map/ppermute | solution.py:20
  219.5 12.2 %all-gather.6.cloned.1.call-done = bf16[32,32,512]{2,0,1:T(8,128)(2,1)} async-done(((bf16[16,32,512]{2,0,1:T(8,128)(2,1)}), bf16[32,32,512]{2,0,1:T(8,128)(2,1)}) %all-gather.6.cloned.1.call-update) | async-done | bytes 1048592 | tf_op jit(solution)/shard_map/all_gather | solution.py:213
  253.0 6.4 %collective-permute-done.6 = bf16[8,1,16,1024]{3,2,0,1:T(8,128)(2,1)S(1)} collective-permute-done((bf16[8,1,16,1024]{3,2,0,1:T(8,128)(2,1)S(1)}, bf16[8,1,16,1024]{3,2,0,1:T(8,128)(2,1)S(1)}, u32[]{:S(2)}, u32[]{:S(2)}) %collective-permute-start.6) | collective-permute-done | bytes 262176 | tf_op jit(solution)/shard_map/ppermute | solution.py:20
  261.9 11.4 %collective-permute-done.7 = bf16[4,2,16,1024]{3,2,0,1:T(8,128)(2,1)S(1)} collective-permute-done((bf16[4,2,16,1024]{3,2,0,1:T(8,128)(2,1)S(1)}, bf16[4,2,16,1024]{3,2,0,1:T(8,128)(2,1)S(1)}, u32[]{:S(2)}, u32[]{:S(2)}) %collective-permute-start.7) | collective-permute-done | bytes 262176 | tf_op jit(solution)/shard_map/ppermute | solution.py:20
  273.4 6.5 %collective-permute-start.8 = (bf16[2,4,16,1024]{3,2,0,1:T(8,128)(2,1)S(1)}, bf16[2,4,16,1024]{3,2,0,1:T(8,128)(2,1)S(1)}, u32[]{:S(2)}, u32[]{:S(2)}) collective-permute-start(bf16[2,4,16,1024]{3,2,0,1:T(8,128)(2,1)S(1)} %get-tuple-element.220), channel_id=1, source_target_pairs={{0,8},{2,10},{4,12},{6,14},{8,0},{10,2},{12,4},{14,6},{16,24},{18,... | collective-permute-start | bytes 786440 | tf_op jit(solution)/shard_map/ppermute | solution.py:20
  279.9 8.8 %collective-permute-done.8 = bf16[2,4,16,1024]{3,2,0,1:T(8,128)(2,1)S(1)} collective-permute-done((bf16[2,4,16,1024]{3,2,0,1:T(8,128)(2,1)S(1)}, bf16[2,4,16,1024]{3,2,0,1:T(8,128)(2,1)S(1)}, u32[]{:S(2)}, u32[]{:S(2)}) %collective-permute-start.8) | collective-permute-done | bytes 262176 | tf_op jit(solution)/shard_map/ppermute | solution.py:20
  311.2 11.4 %collective-permute-start.11 = (bf16[16,8,384]{2,1,0:T(8,128)(2,1)S(1)}, bf16[16,8,384]{2,1,0:T(8,128)(2,1)}, u32[]{:S(2)}, u32[]{:S(2)}) collective-permute-start(bf16[16,8,384]{2,1,0:T(8,128)(2,1)S(1)} %copy.635), channel_id=1, source_target_pairs={{2,0},{4,2},{6,4},{8,6},{10,8},{12,10},{14,12},{16,14},{18,16},{20... | collective-permute-start | bytes 294920 | tf_op jit(solution)/shard_map/ppermute | solution.py:16
  338.3 8.6 %copy.634 = bf16[32,32,512]{1,0,2:T(8,128)(2,1)} copy(bf16[32,32,512]{2,0,1:T(8,128)(2,1)} %all-gather.8.cloned.1.call-done) | data formatting | bytes 2097152 | tf_op jit(solution)/shard_map/all_gather | solution.py:146
  378.5 6.2 %copy.643 = bf16[512,32,32]{0,1,2:T(8,128)(2,1)} copy(bf16[512,32,32]{2,1,0:T(8,128)(2,1)} %gather_fusion.27) | data formatting | bytes 2097152 | tf_op jit(solution)/shard_map/while/body/eval_jaxpr/jit(_take)/gather | solution.py:59
  392.8 6.0 %copy.646 = bf16[512,32,32]{0,1,2:T(8,128)(2,1)} copy(bf16[512,32,32]{2,1,0:T(8,128)(2,1)} %gather_fusion.29) | data formatting | bytes 2097152 | tf_op jit(solution)/shard_map/while/body/eval_jaxpr/jit(_take)/gather | solution.py:59
  405.1 6.0 %copy.649 = bf16[512,32,32]{0,1,2:T(8,128)(2,1)} copy(bf16[512,32,32]{2,1,0:T(8,128)(2,1)} %gather_fusion.31) | data formatting | bytes 2097152 | tf_op jit(solution)/shard_map/while/body/eval_jaxpr/jit(_take)/gather | solution.py:59
  417.4 6.0 %copy.652 = bf16[512,32,32]{0,1,2:T(8,128)(2,1)} copy(bf16[512,32,32]{2,1,0:T(8,128)(2,1)} %gather_fusion.33) | data formatting | bytes 2097152 | tf_op jit(solution)/shard_map/while/body/eval_jaxpr/jit(_take)/gather | solution.py:59
  430.0 6.1 %copy.655 = bf16[512,32,32]{0,1,2:T(8,128)(2,1)} copy(bf16[512,32,32]{2,1,0:T(8,128)(2,1)} %gather_fusion.35) | data formatting | bytes 2097152 | tf_op jit(solution)/shard_map/while/body/eval_jaxpr/jit(_take)/gather | solution.py:59
  462.8 7.6 %collective-permute-start.13 = (bf16[3,8,384]{1,0,2:T(4,128)(2,1)S(1)}, bf16[3,8,384]{1,0,2:T(4,128)(2,1)S(1)}, u32[]{:S(2)}, u32[]{:S(2)}) collective-permute-start(bf16[3,8,384]{1,0,2:T(4,128)(2,1)S(1)} %get-tuple-element.240), channel_id=1, source_target_pairs={{2,0},{4,2},{6,4},{8,6},{10,8},{12,10},{14,12},{16,14},{18,16},{20... | collective-permute-start | bytes 55304 | tf_op jit(solution)/shard_map/ppermute | solution.py:16
  470.4 7.1 %collective-permute-done.12 = bf16[3,8,384]{1,0,2:T(4,128)(2,1)S(1)} collective-permute-done((bf16[3,8,384]{1,0,2:T(4,128)(2,1)S(1)}, bf16[3,8,384]{1,0,2:T(4,128)(2,1)S(1)}, u32[]{:S(2)}, u32[]{:S(2)}) %collective-permute-start.12) | collective-permute-done | bytes 18464 | tf_op jit(solution)/shard_map/ppermute | solution.py:16
  (404 shorter events, 297.4 us)
Async XLA Ops:
  6.5 149.5 %copy-start = (bf16[7,32,32]{2,1,0:T(8,128)(2,1)S(1)}, bf16[7,32,32]{2,1,0:T(8,128)(2,1)}, u32[]{:S(2)}) copy-start(bf16[7,32,32]{2,1,0:T(8,128)(2,1)} %param.65) | copy-start | bytes 43012
  6.5 45.2 %all-gather.4.cloned.1.call-start = ((), (), s32[]{:S(2)}) async-start(), calls=%async_computation | async-start | bytes 1572864 | tf_op jit(solution)/shard_map/all_gather | solution.py:146
  8.7 223.0 %all-gather.6.cloned.1.call-start = ((), (), s32[]{:S(2)}) async-start(), calls=%async_computation.1 | async-start | bytes 1572864 | tf_op jit(solution)/shard_map/all_gather | solution.py:213
  19.0 18.2 %collective-permute-start = (bf16[16,8,384]{2,1,0:T(8,128)(2,1)S(1)}, bf16[16,8,384]{2,1,0:T(8,128)(2,1)S(1)}, u32[]{:S(2)}, u32[]{:S(2)}) collective-permute-start(bf16[16,8,384]{2,1,0:T(8,128)(2,1)S(1)} %copy.585), channel_id=1, source_target_pairs={{0,2},{2,4},{4,6},{6,8},{8,10},{10,12},{12,14},{14,16},{16,18},{18... | collective-permute-start | bytes 294920 | tf_op jit(solution)/shard_map/ppermute | solution.py:16
  23.6 20.5 %collective-permute-start.1 = (bf16[16,8,384]{2,1,0:T(8,128)(2,1)S(1)}, bf16[16,8,384]{2,1,0:T(8,128)(2,1)}, u32[]{:S(2)}, u32[]{:S(2)}) collective-permute-start(bf16[16,8,384]{2,1,0:T(8,128)(2,1)S(1)} %copy.587), channel_id=1, source_target_pairs={{2,0},{4,2},{6,4},{8,6},{10,8},{12,10},{14,12},{16,14},{18,16},{20... | collective-permute-start | bytes 294920 | tf_op jit(solution)/shard_map/ppermute | solution.py:16
  32.5 69.3 %copy-start.32 = (pred[32]{0:T(512)(128)(4,1)}, pred[32]{0:T(512)(128)(4,1)S(1)}, u32[]{:S(2)}) copy-start(pred[32]{0:T(512)(128)(4,1)S(1)} %get-tuple-element.264) | copy-start | bytes 100
  32.5 69.3 %copy-start.34 = (pred[32]{0:T(512)(128)(4,1)}, pred[32]{0:T(512)(128)(4,1)S(1)}, u32[]{:S(2)}) copy-start(pred[32]{0:T(512)(128)(4,1)S(1)} %get-tuple-element.269) | copy-start | bytes 100
  32.5 81.6 %copy-start.36 = (pred[32]{0:T(512)(128)(4,1)}, pred[32]{0:T(512)(128)(4,1)S(1)}, u32[]{:S(2)}) copy-start(pred[32]{0:T(512)(128)(4,1)S(1)} %get-tuple-element.258) | copy-start | bytes 100
  32.5 93.9 %copy-start.26 = (pred[32]{0:T(512)(128)(4,1)}, pred[32]{0:T(512)(128)(4,1)S(1)}, u32[]{:S(2)}) copy-start(pred[32]{0:T(512)(128)(4,1)S(1)} %get-tuple-element.268) | copy-start | bytes 100
  32.5 106.2 %copy-start.28 = (pred[32]{0:T(512)(128)(4,1)}, pred[32]{0:T(512)(128)(4,1)S(1)}, u32[]{:S(2)}) copy-start(pred[32]{0:T(512)(128)(4,1)S(1)} %get-tuple-element.105) | copy-start | bytes 100
  32.5 106.2 %copy-start.30 = (pred[32]{0:T(512)(128)(4,1)}, pred[32]{0:T(512)(128)(4,1)S(1)}, u32[]{:S(2)}) copy-start(pred[32]{0:T(512)(128)(4,1)S(1)} %get-tuple-element.257) | copy-start | bytes 100
  160.5 7.6 %collective-permute-start.2 = (bf16[8,1,16,1024]{3,2,0,1:T(8,128)(2,1)S(1)}, bf16[8,1,16,1024]{3,2,0,1:T(8,128)(2,1)S(1)}, u32[]{:S(2)}, u32[]{:S(2)}) collective-permute-start(bf16[8,1,16,1024]{3,2,0,1:T(8,128)(2,1)S(1)} %get-tuple-element.232), channel_id=1, source_target_pairs={{0,2},{2,0},{4,6},{6,4},{8,10},{10,8},{12,14},{14,12},{16,18},{18,... | collective-permute-start | bytes 786440 | tf_op jit(solution)/shard_map/ppermute | solution.py:20
  168.1 14.8 %collective-permute-start.3 = (bf16[4,2,16,1024]{3,2,0,1:T(8,128)(2,1)S(1)}, bf16[4,2,16,1024]{3,2,0,1:T(8,128)(2,1)S(1)}, u32[]{:S(2)}, u32[]{:S(2)}) collective-permute-start(bf16[4,2,16,1024]{3,2,0,1:T(8,128)(2,1)S(1)} %get-tuple-element.230), channel_id=1, source_target_pairs={{0,4},{2,6},{4,0},{6,2},{8,12},{10,14},{12,8},{14,10},{16,20},{18,... | collective-permute-start | bytes 786440 | tf_op jit(solution)/shard_map/ppermute | solution.py:20
  183.0 16.6 %collective-permute-start.4 = (bf16[2,4,16,1024]{3,2,0,1:T(8,128)(2,1)S(1)}, bf16[2,4,16,1024]{3,2,0,1:T(8,128)(2,1)S(1)}, u32[]{:S(2)}, u32[]{:S(2)}) collective-permute-start(bf16[2,4,16,1024]{3,2,0,1:T(8,128)(2,1)S(1)} %get-tuple-element.228), channel_id=1, source_target_pairs={{0,8},{2,10},{4,12},{6,14},{8,0},{10,2},{12,4},{14,6},{16,24},{18,... | collective-permute-start | bytes 786440 | tf_op jit(solution)/shard_map/ppermute | solution.py:20
  199.8 7.5 %collective-permute-start.5 = (bf16[1,8,16,1024]{3,2,1,0:T(8,128)(2,1)S(1)}, bf16[1,8,16,1024]{3,2,1,0:T(8,128)(2,1)S(1)}, u32[]{:S(2)}, u32[]{:S(2)}) collective-permute-start(bf16[1,8,16,1024]{3,2,1,0:T(8,128)(2,1)S(1)} %get-tuple-element.226), channel_id=1, source_target_pairs={{0,16},{2,18},{4,20},{6,22},{8,24},{10,26},{12,28},{14,30},{16,0},... | collective-permute-start | bytes 786440 | tf_op jit(solution)/shard_map/ppermute | solution.py:20
  219.2 119.1 %all-gather.8.cloned.1.call-start = ((), (), s32[]{:S(2)}) async-start(), calls=%async_computation.2 | async-start | bytes 1572864 | tf_op jit(solution)/shard_map/all_gather | solution.py:146
  251.7 7.8 %collective-permute-start.6 = (bf16[8,1,16,1024]{3,2,0,1:T(8,128)(2,1)S(1)}, bf16[8,1,16,1024]{3,2,0,1:T(8,128)(2,1)S(1)}, u32[]{:S(2)}, u32[]{:S(2)}) collective-permute-start(bf16[8,1,16,1024]{3,2,0,1:T(8,128)(2,1)S(1)} %get-tuple-element.224), channel_id=1, source_target_pairs={{0,2},{2,0},{4,6},{6,4},{8,10},{10,8},{12,14},{14,12},{16,18},{18,... | collective-permute-start | bytes 786440 | tf_op jit(solution)/shard_map/ppermute | solution.py:20
  259.5 13.8 %collective-permute-start.7 = (bf16[4,2,16,1024]{3,2,0,1:T(8,128)(2,1)S(1)}, bf16[4,2,16,1024]{3,2,0,1:T(8,128)(2,1)S(1)}, u32[]{:S(2)}, u32[]{:S(2)}) collective-permute-start(bf16[4,2,16,1024]{3,2,0,1:T(8,128)(2,1)S(1)} %get-tuple-element.222), channel_id=1, source_target_pairs={{0,4},{2,6},{4,0},{6,2},{8,12},{10,14},{12,8},{14,10},{16,20},{18,... | collective-permute-start | bytes 786440 | tf_op jit(solution)/shard_map/ppermute | solution.py:20
  273.4 15.3 %collective-permute-start.8 = (bf16[2,4,16,1024]{3,2,0,1:T(8,128)(2,1)S(1)}, bf16[2,4,16,1024]{3,2,0,1:T(8,128)(2,1)S(1)}, u32[]{:S(2)}, u32[]{:S(2)}) collective-permute-start(bf16[2,4,16,1024]{3,2,0,1:T(8,128)(2,1)S(1)} %get-tuple-element.220), channel_id=1, source_target_pairs={{0,8},{2,10},{4,12},{6,14},{8,0},{10,2},{12,4},{14,6},{16,24},{18,... | collective-permute-start | bytes 786440 | tf_op jit(solution)/shard_map/ppermute | solution.py:20
  288.9 5.5 %collective-permute-start.9 = (bf16[1,8,16,1024]{3,2,1,0:T(8,128)(2,1)S(1)}, bf16[1,8,16,1024]{3,2,1,0:T(8,128)(2,1)S(1)}, u32[]{:S(2)}, u32[]{:S(2)}) collective-permute-start(bf16[1,8,16,1024]{3,2,1,0:T(8,128)(2,1)S(1)} %get-tuple-element.218), channel_id=1, source_target_pairs={{0,16},{2,18},{4,20},{6,22},{8,24},{10,26},{12,28},{14,30},{16,0},... | collective-permute-start | bytes 786440 | tf_op jit(solution)/shard_map/ppermute | solution.py:20
  308.2 14.5 %collective-permute-start.10 = (bf16[16,8,384]{2,1,0:T(8,128)(2,1)S(1)}, bf16[16,8,384]{2,1,0:T(8,128)(2,1)S(1)}, u32[]{:S(2)}, u32[]{:S(2)}) collective-permute-start(bf16[16,8,384]{2,1,0:T(8,128)(2,1)S(1)} %copy.633), channel_id=1, source_target_pairs={{0,2},{2,4},{4,6},{6,8},{8,10},{10,12},{12,14},{14,16},{16,18},{18... | collective-permute-start | bytes 294920 | tf_op jit(solution)/shard_map/ppermute | solution.py:16
  311.2 19.5 %collective-permute-start.11 = (bf16[16,8,384]{2,1,0:T(8,128)(2,1)S(1)}, bf16[16,8,384]{2,1,0:T(8,128)(2,1)}, u32[]{:S(2)}, u32[]{:S(2)}) collective-permute-start(bf16[16,8,384]{2,1,0:T(8,128)(2,1)S(1)} %copy.635), channel_id=1, source_target_pairs={{2,0},{4,2},{6,4},{8,6},{10,8},{12,10},{14,12},{16,14},{18,16},{20... | collective-permute-start | bytes 294920 | tf_op jit(solution)/shard_map/ppermute | solution.py:16
  460.8 16.7 %collective-permute-start.12 = (bf16[3,8,384]{1,0,2:T(4,128)(2,1)S(1)}, bf16[3,8,384]{1,0,2:T(4,128)(2,1)S(1)}, u32[]{:S(2)}, u32[]{:S(2)}) collective-permute-start(bf16[3,8,384]{1,0,2:T(4,128)(2,1)S(1)} %get-tuple-element.239), channel_id=1, source_target_pairs={{0,2},{2,4},{4,6},{6,8},{8,10},{10,12},{12,14},{14,16},{16,18},{18... | collective-permute-start | bytes 55304 | tf_op jit(solution)/shard_map/ppermute | solution.py:16
  462.8 15.6 %collective-permute-start.13 = (bf16[3,8,384]{1,0,2:T(4,128)(2,1)S(1)}, bf16[3,8,384]{1,0,2:T(4,128)(2,1)S(1)}, u32[]{:S(2)}, u32[]{:S(2)}) collective-permute-start(bf16[3,8,384]{1,0,2:T(4,128)(2,1)S(1)} %get-tuple-element.240), channel_id=1, source_target_pairs={{2,0},{4,2},{6,4},{8,6},{10,8},{12,10},{14,12},{16,14},{18,16},{20... | collective-permute-start | bytes 55304 | tf_op jit(solution)/shard_map/ppermute | solution.py:16
  (60 other events, 535.9 us)
Sparse Core Ops, SparseCore 0:
  9.2 17.5 all-gather.3
  219.3 12.3 all-gather.5
  297.3 19.0 all-gather.7
where the time goes:
time: 516 us; the launch traced here: 509 us
  local copies, waits for them, and re-layouts  286 us (55%)
  waiting for transfers between devices  95.2 us (18%)
  starting transfers between devices  48.8 us (9%)
  other arithmetic  39.9 us (8%)
  blocking collectives  15.5 us (3%)
  between operations  15.5 us (3%)
  matrix products  8.32 us (2%)
    gather x36, local copies, waits for them, and re-layouts, make_taps(): face_fill = jnp.take(near_faces[direction], facepos[which_axis], axis=2)  129 us
    ppermute x8, waiting for transfers between devices, swapped(): lax.ppermute(shard, axis, [(i, i ^ 1 << stride) for i in range(lax.axis_s...  75 us
    ppermute x6, starting transfers between devices, shifted(): lax.ppermute(value, axis, [(source, source + steps) for source in range(f...  34.5 us
    slice x21, local copies, waits for them, and re-layouts, neighbour_faces(): face_pool[:, :, opposite * 64:(opposite + 1) * 64]  18.8 us
    all_gather x2, local copies, waits for them, and re-layouts, fine_conv(): lax.all_gather(xlocal, 'chan', axis=0, tiled=True)  17.1 us
    gather x18, local copies, waits for them, and re-layouts, neighbour_faces(): jnp.take(face_pool[:, :, opposite * 64:(opposite + 1) * 64], jnp.where(pr...  16.5 us
    unnamed x17, other arithmetic  14.1 us
    ppermute x8, starting transfers between devices, swapped(): lax.ppermute(shard, axis, [(i, i ^ 1 << stride) for i in range(lax.axis_s...  14 us
  transfers between devices with their start and end apart: 17, of which 11 were waited for; matrix products, arithmetic and copies ran while one was open for 9% of the time, Pallas kernels for 0%

commit v1 on v0

v1 whole, which is shorter than its diff:
```python
import functools

import jax
import jax.numpy as jnp
from jax import lax
from jax.experimental import pallas as pl
from jax.experimental.pallas import tpu as pltpu
from jax.sharding import PartitionSpec as P

BF = jnp.bfloat16
F32 = jnp.float32
WINDOW = 16
ABSENT = 40
NT = (((1,), (1,)), ((), ()))


def iota(shape, dim):
    return lax.broadcasted_iota(jnp.int32, shape, dim)


def dot(a, b):
    return jnp.dot(a, b, preferred_element_type=F32)


def shifts(own, nb):
    lane = iota(own[0].shape, 1)
    low, j, k = lane < 64, (lane >> 3) & 7, lane & 7
    turn = lambda x, steps: pltpu.roll(x, steps, 1)
    half = [turn(x, 64) for x in own]
    minus, plus = turn(nb(0, 3), 64), turn(nb(1, 0), 64)
    four = range(4)
    return [
        [jnp.where(low, half[q - 1] if q else minus, half[q]) for q in four],
        [jnp.where(low, half[q], half[q + 1] if q < 3 else plus) for q in four],
        [jnp.where(j == 0, turn(nb(2, q), 72), turn(own[q], 8)) for q in four],
        [jnp.where(j == 7, turn(nb(3, q), 56), turn(own[q], 120)) for q in four],
        [jnp.where(k == 0, turn(nb(4, q), 121), turn(own[q], 1)) for q in four],
        [jnp.where(k == 7, turn(nb(5, q), 7), turn(own[q], 127)) for q in four],
    ]


def quarters(x):
    return [x[:, 128 * q : 128 * q + 128] for q in range(4)]


def conv(own, nb, weight, bias):
    fields = [own] + shifts(own, nb)
    taps = jnp.concatenate([jnp.concatenate(f, axis=1) for f in fields], axis=0)
    u = dot(weight, taps) + bias
    return (0.5 * u * (1.0 + jnp.tanh(0.5 * u))).astype(BF)


def kernel(
    feat, cfield, nb_s, nb_v, oct_s, own_s, ew, eb, cw, cb, dw, db, psi,
    vel,
    fv, cv, pool_e, near_e, ct, fr, fsel, fsend, enc, pooled, eup, pool_d, near_d, dec, sp,
    perm, pmat, umat, wt, bt, psib, inv,
    load_sem, ce_s, ce_r, fe_s, fe_r, aa_s, aa_r, fx_s, fx_r, cd_s, cd_r, fd_s, fd_r, st_s, st_r,
):
    s, h = lax.axis_index("space"), lax.axis_index("chan")
    count = lax.axis_size("space")
    pos = s % WINDOW
    base = s - pos
    other = (s, 1 - h)
    after, before = (s + 1) % count, (s + count - 1) % count
    ch = pl.ds(pl.multiple_of(16 * h, 16), 16)

    def send(src, dst, ssem, rsem, device):
        return pltpu.make_async_remote_copy(
            src_ref=src, dst_ref=dst, send_sem=ssem, recv_sem=rsem,
            device_id=device, device_id_type=pl.DeviceIdType.MESH,
        )

    load_f = pltpu.make_async_copy(feat, fv, load_sem.at[0])
    load_c = pltpu.make_async_copy(cfield, cv, load_sem.at[1])
    load_f.start()
    load_c.start()

    barrier = pltpu.get_barrier_semaphore()
    peers = [(base + (pos + o) % WINDOW, h) for o in range(1, WINDOW)]
    everyone = peers + [other, (after, 0), (after, 1), (before, 0), (before, 1)]
    for device in everyone:
        pl.semaphore_signal(barrier, inc=1, device_id=device, device_id_type=pl.DeviceIdType.MESH)

    r, q = iota((256, 256), 0), iota((256, 256), 1)
    perm[...] = (q == (r & 15) * 16 + (r >> 4)).astype(BF)

    def cell(v):
        return ((v >> 7) << 6) + (((v >> 4) & 3) << 3) + ((v >> 1) & 3)

    pmat[...] = jnp.where(cell(iota((512, 256), 0)) == iota((512, 256), 1), 0.125, 0.0).astype(BF)
    umat[...] = (iota((256, 512), 0) == cell(iota((256, 512), 1))).astype(BF)
    eye = (iota((32, 32), 0) == iota((32, 32), 1)).astype(BF)
    for n, (w, b) in enumerate(((ew, eb), (cw, cb), (dw, db))):
        flat = w[...].reshape(224, 32)
        wt[n] = lax.dot_general(eye, flat, NT, preferred_element_type=F32).astype(BF)
        spread = jnp.where(iota((32, 32), 0) == iota((32, 32), 1), b[...], 0.0)
        bt[n] = jnp.broadcast_to(jnp.sum(spread, axis=1, keepdims=True), (32, 128))
    rows, lanes = iota((48, 512), 0), iota((48, 512), 1)
    tile = (iota((32, 512), 0) == (iota((32, 512), 1) & 31)).astype(BF)
    wide = lax.dot_general(
        psi[...], tile, (((0,), (0,)), ((), ())), preferred_element_type=F32
    )
    pick = jnp.concatenate([jnp.broadcast_to(wide[m : m + 1], (16, 512)) for m in range(3)], axis=0)
    psib[...] = jnp.where((rows & 15) == (lanes >> 5), pick, 0.0).astype(BF)
    pool_e[ABSENT] = jnp.zeros((32, 512), BF)
    pool_d[ABSENT] = jnp.zeros((32, 512), BF)
    for kl in range(2):
        for o in range(8):
            found = jnp.int32(0)
            for child in range(8):
                hit = oct_s[16 * h + 8 * kl + child] == o
                found = jnp.where(hit, jnp.int32(8 * kl + child), found)
            inv[8 * kl + o] = found

    pl.semaphore_wait(barrier, len(everyone))

    load_f.wait()
    for g in range(2):
        part = fv[:, 16 * g : 16 * g + 16, :].reshape(256, 512)
        pool_e[16 * g : 16 * g + 16, ch, :] = dot(perm[...], part).astype(BF).reshape(16, 16, 512)
    face_up = send(pool_e.at[24:32, ch], near_e.at[:, ch], fe_s.at[0], fe_r.at[h], (after, 0))
    face_down = send(pool_e.at[0:8, ch], near_e.at[:, ch], fe_s.at[1], fe_r.at[h], (before, 1))
    both = send(pool_e.at[0:32, ch], pool_e.at[0:32, ch], ce_s, ce_r, other)
    face_up.start()
    face_down.start()
    both.start()

    load_c.wait()
    for g in range(2):
        part = cv[:, 16 * g : 16 * g + 16, :].reshape(256, 512)
        ct[16 * g : 16 * g + 16] = dot(perm[...], part).astype(BF).reshape(16, 16, 512)
    spread_out = []
    for o in range(1, WINDOW):
        to = (pos + o) % WINDOW
        copy = send(
            ct.at[pl.ds(2 * to, 2)], fr.at[pl.ds(2 * pos, 2)], aa_s.at[o], aa_r.at[o], (base + to, h)
        )
        copy.start()
        spread_out.append(copy)
    fr[pl.ds(2 * pos, 2)] = ct[pl.ds(2 * pos, 2)]

    def fine(pool, n, out, first):
        weight, bias = wt[n], bt[n][:, :1]

        def body(t, carry):
            local = first + t
            row = 16 * h + local

            def spot(d):
                at = nb_s[row, d]
                rel = at - 32 * s
                return jnp.where(at < 0, ABSENT, rel & 63)

            spots = [spot(d) for d in range(6)]
            nb = lambda d, q: pool[spots[d], :, 128 * q : 128 * q + 128]
            out[local] = conv(quarters(pool[row]), nb, weight, bias)
            return carry

        lax.fori_loop(0, 8, body, 0)

    def pool_half(first):
        rows = enc[pl.ds(first, 8)].reshape(256, 512)
        pooled[pl.ds(first, 8)] = dot(rows, pmat[...]).astype(BF).reshape(8, 32, 256)

    inner, edge = 8 * (1 - h), 8 * h
    near = pl.ds(32 + 24 * (1 - h), 8)
    both.wait_recv()
    fine(pool_e, 0, enc, inner)
    pool_half(inner)
    for c in range(2):
        chc = pl.ds(16 * c, 16)
        send(pool_e.at[24:32, chc], near_e.at[:, chc], fe_s.at[0], fe_r.at[c], (after, 0)).wait_recv()
    pool_e[near, :, :] = near_e[...]
    fine(pool_e, 0, enc, edge)
    pool_half(edge)

    for copy in spread_out:
        copy.wait_recv()
    ow = [own_s[n, 0] for n in range(4)]
    slot = []
    for n in range(4):
        rank = jnp.int32(0)
        for m in range(n):
            rank = rank + jnp.where(ow[m] == ow[n], 1, 0)
        slot.append(2 * ow[n] + rank)
    for kl in range(2):
        mine = jnp.where(h == 0, slot[kl], slot[2 + kl])
        theirs = jnp.where(h == 0, slot[2 + kl], slot[kl])
        fsend[kl] = fr[theirs]
        fsel[kl, ch, :] = fr[mine]
    swap = send(fsend, fsel.at[:, ch], fx_s, fx_r, other)
    swap.start()

    gathered = []
    for kl in range(2):
        acc = [None, None]
        for o in range(8):
            part = pooled[inv[8 * kl + o]]
            step = 32 * ((o >> 1) & 1) + 4 * (o & 1)
            part = pltpu.roll(part, step, 1) if step else part
            acc[o >> 2] = part if acc[o >> 2] is None else acc[o >> 2] + part
        gathered.append(jnp.concatenate(acc, axis=1))
    swap.wait_recv()
    nothing = jnp.zeros((32, 128), BF)
    for kl in range(2):
        cin = (gathered[kl].astype(F32) + fsel[kl].astype(F32)).astype(BF)
        cout = conv(quarters(cin), lambda d, q: nothing, wt[1], bt[1][:, :1])
        parts = []
        for o in range(8):
            part = cout[:, 256 * (o >> 2) : 256 * (o >> 2) + 256]
            step = 32 * ((o >> 1) & 1) + 4 * (o & 1)
            parts.append(pltpu.roll(part, 256 - step, 1) if step else part)
        up = dot(jnp.concatenate(parts, axis=0), umat[...])
        eup[8 * kl : 8 * kl + 8] = up.astype(BF).reshape(8, 32, 512)

    def decoder_in(first):
        def body(t, carry):
            local = first + t
            row = 16 * h + local
            up = eup[first + oct_s[row]]
            pool_d[row] = (enc[local].astype(F32) + up.astype(F32)).astype(BF)
            return carry

        lax.fori_loop(0, 8, body, 0)

    partner = ((s + 2 * h - 1 + count) % count, 1 - h)
    decoder_in(edge)
    edge_rows = pl.ds(16 * h + edge, 8)
    face_d = send(pool_d.at[edge_rows], near_d, fd_s, fd_r, partner)
    face_d.start()
    cross = [send(pool_d.at[edge_rows], pool_d.at[edge_rows], cd_s.at[0], cd_r.at[0], other)]
    cross[0].start()
    decoder_in(inner)
    inner_rows = pl.ds(16 * h + inner, 8)
    cross.append(send(pool_d.at[inner_rows], pool_d.at[inner_rows], cd_s.at[1], cd_r.at[1], other))
    cross[1].start()
    cross[0].wait_recv()
    cross[1].wait_recv()
    fine(pool_d, 2, dec, inner)
    face_d.wait_recv()
    pool_d[near, :, :] = near_d[...]
    fine(pool_d, 2, dec, edge)

    stream = dot(psib[...], dec[...].reshape(512, 512)).astype(BF).reshape(3, 16, 512)
    own_rows = pl.ds(pl.multiple_of(16 + 16 * h, 16), 16)
    sp[:, own_rows, :] = stream
    side = s + 2 * h - 1 + count
    far = pl.ds(pl.multiple_of(48 * (1 - h), 16), 16)
    outgoing = [send(sp.at[:, own_rows], sp.at[:, far], st_s.at[1 + c], st_r.at[2 - h], (side % count, c)) for c in range(2)]
    outgoing.append(send(sp.at[:, own_rows], sp.at[:, own_rows], st_s.at[0], st_r.at[0], other))
    for copy in outgoing:
        copy.start()
    hots = []
    for d in range(6):
        at = nb_v[:, d : d + 1]
        rel = jnp.where(at < 0, -1, at - 32 * s + 16)
        hots.append((iota((32, 64), 1) == rel).astype(BF))
    outgoing[2].wait_recv()
    for n in range(1, 3):
        send(sp.at[:, own_rows], sp.at[:, far], st_s.at[n], st_r.at[n], other).wait_recv()

    diff = {}
    for m in range(3):
        axes = [a for a in range(3) if a != m]
        hot = jnp.concatenate([hots[2 * a + side_] for a in axes for side_ in range(2)], axis=0)
        faces = dot(hot, sp[m])
        own = quarters(sp[m, 16:48].astype(F32))
        pieces = {2 * a + e: quarters(faces[64 * n + 32 * e : 64 * n + 32 * e + 32]) for n, a in enumerate(axes) for e in range(2)}
        got = shifts(own, lambda d, q: pieces[d][q] if d in pieces else own[q])
        for a in axes:
            diff[a, m] = [0.5 * (x - y) for x, y in zip(got[2 * a + 1], got[2 * a])]
    for m in range(3):
        a, b = (m + 1) % 3, (m + 2) % 3
        vel[m] = jnp.concatenate([x - y for x, y in zip(diff[a, b], diff[b, a])], axis=1)

    face_up.wait_send()
    face_down.wait_send()
    both.wait_send()
    for copy in spread_out:
        copy.wait_send()
    swap.wait_send()
    face_d.wait_send()
    for copy in cross + outgoing:
        copy.wait_send()


def on_device(features, neighbours, octants, owners, coarse_field, ew, eb, cw, cb, dw, db, psi):
    vmem = pl.BlockSpec(memory_space=pltpu.VMEM)
    smem = pl.BlockSpec(memory_space=pltpu.SMEM)
    hbm = pl.BlockSpec(memory_space=pl.ANY)
    dma = pltpu.SemaphoreType.DMA
    v = lambda *shape: pltpu.VMEM(shape, BF)
    return pl.pallas_call(
        kernel,
        out_shape=jax.ShapeDtypeStruct((3, 32, 512), F32),
        in_specs=[hbm, hbm, smem, vmem, smem, smem] + [vmem] * 7,
        out_specs=vmem,
        scratch_shapes=[
            v(16, 32, 512), v(16, 32, 512), v(64, 32, 512), v(8, 32, 512),
            v(32, 16, 512), v(32, 16, 512), v(2, 32, 512), v(2, 16, 512),
            v(16, 32, 512), v(16, 32, 256), v(16, 32, 512), v(64, 32, 512), v(8, 32, 512),
            v(16, 32, 512), v(3, 64, 512),
            v(256, 256), v(512, 256), v(256, 512), v(3, 32, 224), pltpu.VMEM((3, 32, 128), F32),
            v(48, 512), pltpu.SMEM((16,), jnp.int32),
            dma((2,)), dma, dma, dma((2,)), dma((2,)), dma((16,)), dma((16,)), dma, dma,
            dma((2,)), dma((2,)), dma, dma, dma((3,)), dma((3,)),
        ],
        compiler_params=pltpu.CompilerParams(
            collective_id=0, has_side_effects=True, vmem_limit_bytes=48 * 1024 * 1024
        ),
    )(
        features, coarse_field, neighbours, neighbours, octants, owners,
        ew, eb.reshape(1, 32), cw, cb.reshape(1, 32), dw, db.reshape(1, 32), psi,
    )


def solution(mesh):
    split, rows = P("chan", "space", None), P("space", None)
    return jax.shard_map(
        on_device,
        mesh=mesh,
        in_specs=(split, rows, P("space"), rows, split) + (P(),) * 7,
        out_specs=P(None, "space", None),
        check_vma=False,
    )
```

time: 516 us -> 51.9 us (0.10)
  the two profiles are of different devices: /device:TPU:25 before, /device:TPU:1 now
where the time goes in v1:
time: 51.9 us; the launch traced here: 51.5 us
  Pallas kernels  43.5 us (84%)
  local copies, waits for them, and re-layouts  7.93 us (15%)
    pallas_call x1, Pallas kernels, on_device(): pl.pallas_call(kernel, out_shape=jax.ShapeDtypeStruct((3, 32, 512), F32),...  43.5 us
    unnamed x28, local copies, waits for them, and re-layouts  7.93 us

profile of v1, /device:TPU:1, one launch (start us, length us, event | category | flops | bytes accessed | tf_op | source)
XLA Modules:
  0.0 51.5 jit_solution(12480146322458615861)
XLA Ops:
  0.0 0.0 copy-start.11
  0.0 0.7 %copy-done.11 = s32[4,1]{0,1:T(1,128)S(1)} copy-done((s32[4,1]{0,1:T(1,128)S(1)}, s32[4,1]{0,1:T(1,128)}, u32[]{:S(2)}) %copy-start.11) | copy-done | bytes 40
  0.7 0.0 copy-start.10
  0.7 0.1 copy.15.own_s
  0.8 0.6 %copy-done.10 = bf16[32,3]{0,1:T(4,128)(2,1)S(1)} copy-done((bf16[32,3]{0,1:T(4,128)(2,1)S(1)}, bf16[32,3]{0,1:T(4,128)(2,1)}, u32[]{:S(2)}) %copy-start.10) | copy-done | bytes 216
  1.3 0.0 copy-start.9
  1.3 0.1 copy.16.psi
  1.4 0.6 %copy-done.9 = s32[32,6]{0,1:T(8,128)S(1)} copy-done((s32[32,6]{0,1:T(8,128)S(1)}, s32[32,6]{0,1:T(8,128)}, u32[]{:S(2)}) %copy-start.9) | copy-done | bytes 792
  2.0 0.0 copy-start.5
  2.0 0.0 copy-start.7
  2.0 0.0 copy-start.8
  2.0 0.1 copy.13.nb_s.nb_v
  2.1 0.6 %copy-done.5 = s32[32]{0:T(128)S(1)} copy-done((s32[32]{0:T(128)S(1)}, s32[32]{0:T(128)}, u32[]{:S(2)}) %copy-start.5) | copy-done | bytes 152
  2.7 0.0 copy-done.6
  2.7 0.0 copy-done.7
  2.7 0.0 copy-done.8
  2.7 0.0 copy-start
  2.7 1.0 %copy-done = bf16[16,32,512]{2,1,0:T(8,128)(2,1)S(1)} copy-done((bf16[16,32,512]{2,1,0:T(8,128)(2,1)S(1)}, bf16[16,32,512]{2,1,0:T(8,128)(2,1)}, u32[]{:S(2)}) %copy-start) | copy-done | bytes 524312
  3.8 1.0 %copy-done.1 = bf16[16,32,512]{2,1,0:T(8,128)(2,1)S(1)} copy-done((bf16[16,32,512]{2,1,0:T(8,128)(2,1)S(1)}, bf16[16,32,512]{2,1,0:T(8,128)(2,1)}, u32[]{:S(2)}) %copy-start.1) | copy-done | bytes 524312
  4.8 0.8 %copy-done.2 = bf16[7,32,32]{2,1,0:T(8,128)(2,1)S(1)} copy-done((bf16[7,32,32]{2,1,0:T(8,128)(2,1)S(1)}, bf16[7,32,32]{2,1,0:T(8,128)(2,1)}, u32[]{:S(2)}) %copy-start.2) | copy-done | bytes 14360
  5.6 0.8 %copy-done.3 = bf16[7,32,32]{2,1,0:T(8,128)(2,1)S(1)} copy-done((bf16[7,32,32]{2,1,0:T(8,128)(2,1)S(1)}, bf16[7,32,32]{2,1,0:T(8,128)(2,1)}, u32[]{:S(2)}) %copy-start.3) | copy-done | bytes 14360
  6.5 0.8 %copy-done.4 = bf16[7,32,32]{2,1,0:T(8,128)(2,1)S(1)} copy-done((bf16[7,32,32]{2,1,0:T(8,128)(2,1)S(1)}, bf16[7,32,32]{2,1,0:T(8,128)(2,1)}, u32[]{:S(2)}) %copy-start.4) | copy-done | bytes 14360
  7.3 43.5 %shard_map.118 = f32[3,32,512]{2,1,0:T(8,128)S(1)} custom-call(bf16[16,32,512]{2,1,0:T(8,128)(2,1)S(1)} %copy-done, bf16[16,32,512]{2,1,0:T(8,128)(2,1)S(1)} %copy-done.1, s32[32,6]{1,0:T(8,128)S(1)} %copy.13.nb_s.nb_v, s32[32,6]{1,0:T(8,128)S(1)} %copy.13.nb_s.nb_v, s32[32]{0:T(128)S(1)} %copy-done.5, s32[4,1]{1,0:T(4,128)S(1)} %copy.15.own_s, ...), custom_call_target="tpu_custom_call" | custom-call | tf_op jit(solution)/shard_map/pallas_call | solution.py:294
  50.8 0.7 %copy.18 = f32[3,32,512]{2,1,0:T(8,128)} copy(f32[3,32,512]{2,1,0:T(8,128)S(1)} %shard_map.118) | data formatting | bytes 393216
  (5 shorter events, 0.0 us)
Async XLA Ops:
  0.0 0.7 %copy-start.11 = (s32[4,1]{0,1:T(1,128)S(1)}, s32[4,1]{0,1:T(1,128)}, u32[]{:S(2)}) copy-start(s32[4,1]{0,1:T(1,128)} %param.15) | copy-start | bytes 52
  0.7 0.7 %copy-start.10 = (bf16[32,3]{0,1:T(4,128)(2,1)S(1)}, bf16[32,3]{0,1:T(4,128)(2,1)}, u32[]{:S(2)}) copy-start(bf16[32,3]{0,1:T(4,128)(2,1)} %param.23) | copy-start | bytes 580
  1.3 0.7 %copy-start.9 = (s32[32,6]{0,1:T(8,128)S(1)}, s32[32,6]{0,1:T(8,128)}, u32[]{:S(2)}) copy-start(s32[32,6]{0,1:T(8,128)} %param.13) | copy-start | bytes 2308
  2.0 0.7 %copy-start.5 = (s32[32]{0:T(128)S(1)}, s32[32]{0:T(128)}, u32[]{:S(2)}) copy-start(s32[32]{0:T(128)} %oct_s.1) | copy-start | bytes 388
  2.0 0.7 %copy-start.6 = (f32[32]{0:T(128)S(1)}, f32[32]{0:T(128)}, u32[]{:S(2)}) copy-start(f32[32]{0:T(128)} %param.18) | copy-start | bytes 388
  2.0 0.7 %copy-start.7 = (f32[32]{0:T(128)S(1)}, f32[32]{0:T(128)}, u32[]{:S(2)}) copy-start(f32[32]{0:T(128)} %param.20) | copy-start | bytes 388
  2.0 0.7 %copy-start.8 = (f32[32]{0:T(128)S(1)}, f32[32]{0:T(128)}, u32[]{:S(2)}) copy-start(f32[32]{0:T(128)} %param.22) | copy-start | bytes 388
  2.7 1.0 %copy-start = (bf16[16,32,512]{2,1,0:T(8,128)(2,1)S(1)}, bf16[16,32,512]{2,1,0:T(8,128)(2,1)}, u32[]{:S(2)}) copy-start(bf16[16,32,512]{2,1,0:T(8,128)(2,1)} %feat.1) | copy-start | bytes 1572868
  3.8 1.0 %copy-start.1 = (bf16[16,32,512]{2,1,0:T(8,128)(2,1)S(1)}, bf16[16,32,512]{2,1,0:T(8,128)(2,1)}, u32[]{:S(2)}) copy-start(bf16[16,32,512]{2,1,0:T(8,128)(2,1)} %cfield.1) | copy-start | bytes 1572868
  4.8 0.8 %copy-start.2 = (bf16[7,32,32]{2,1,0:T(8,128)(2,1)S(1)}, bf16[7,32,32]{2,1,0:T(8,128)(2,1)}, u32[]{:S(2)}) copy-start(bf16[7,32,32]{2,1,0:T(8,128)(2,1)} %ew.1) | copy-start | bytes 43012
  5.6 0.8 %copy-start.3 = (bf16[7,32,32]{2,1,0:T(8,128)(2,1)S(1)}, bf16[7,32,32]{2,1,0:T(8,128)(2,1)}, u32[]{:S(2)}) copy-start(bf16[7,32,32]{2,1,0:T(8,128)(2,1)} %cw.1) | copy-start | bytes 43012
  6.4 0.8 %copy-start.4 = (bf16[7,32,32]{2,1,0:T(8,128)(2,1)S(1)}, bf16[7,32,32]{2,1,0:T(8,128)(2,1)}, u32[]{:S(2)}) copy-start(bf16[7,32,32]{2,1,0:T(8,128)(2,1)} %dw.1) | copy-start | bytes 43012

commit v2 on v1

v2 whole, which is shorter than its diff:
```python
import jax
import jax.numpy as jnp
import numpy as np
from jax import lax
from jax.experimental import pallas as pl
from jax.experimental.pallas import tpu as pltpu
from jax.sharding import PartitionSpec as P

BF = jnp.bfloat16
F32 = jnp.float32
WINDOW = 16
ABSENT = 40
NT = (((1,), (1,)), ((), ()))


def tables():
    r = np.arange(256)
    perm = (r[:, None] % 16 * 16 + r[:, None] // 16 == r[None]).astype(np.float32)
    v = np.arange(512)
    i, j, k = v // 64, v // 8 % 8, v % 8
    cell = i // 2 * 64 + j // 2 * 8 + k // 2
    place = (cell[:, None] == r[None]).astype(np.float32)
    faces = np.zeros((2, 512, 256), np.float32)
    for n, end in enumerate((0, 7)):
        on_i, on_j, on_k = i == end, j == end, k == end
        faces[n, v[on_i], (j * 8 + k)[on_i]] = 1
        on_j &= ~on_i
        faces[n, v[on_j], 64 + (i * 8 + k)[on_j]] = 1
        on_k &= ~(i == end) & ~(j == end)
        faces[n, v[on_k], 128 + (i * 8 + j)[on_k]] = 1
    return [jnp.asarray(m, BF) for m in (perm, 0.125 * place, place.T, faces)]


def iota(shape, dim):
    return lax.broadcasted_iota(jnp.int32, shape, dim)


def dot(a, b):
    return jnp.dot(a, b, preferred_element_type=F32)


def shifts(own, nb):
    lane = iota(own[0].shape, 1)
    low, j, k = lane < 64, (lane >> 3) & 7, lane & 7
    turn = lambda x, steps: pltpu.roll(x, steps, 1)
    half = [turn(x, 64) for x in own]
    minus, plus = turn(nb(0, 3), 64), turn(nb(1, 0), 64)
    four = range(4)
    return [
        [jnp.where(low, half[q - 1] if q else minus, half[q]) for q in four],
        [jnp.where(low, half[q], half[q + 1] if q < 3 else plus) for q in four],
        [jnp.where(j == 0, turn(nb(2, q), 72), turn(own[q], 8)) for q in four],
        [jnp.where(j == 7, turn(nb(3, q), 56), turn(own[q], 120)) for q in four],
        [jnp.where(k == 0, turn(nb(4, q), 121), turn(own[q], 1)) for q in four],
        [jnp.where(k == 7, turn(nb(5, q), 7), turn(own[q], 127)) for q in four],
    ]


def quarters(x):
    return [x[:, 128 * q : 128 * q + 128] for q in range(4)]


def conv(own, nb, weight, bias):
    fields = [own] + shifts(own, nb)
    taps = jnp.concatenate([jnp.concatenate(f, axis=1) for f in fields], axis=0)
    u = dot(weight, taps) + bias
    return (0.5 * u * (1.0 + jnp.tanh(0.5 * u))).astype(BF)


def kernel(
    feat, cfield, nb_h, oct_h, own_h, ew_h, eb_h, cw_h, cb_h, dw_h, db_h, psi_h,
    perm_h, pmat_h, umat_h, face_h,
    vel_h,
    nb_s, oct_s, own_s, nb_v, ew, eb, cw, cb, dw, db, psi, vel, fv, cv, pool_e, pe, qe, ct, fr, fsel, fsend, enc, pooled, eup, pool_d, pd, qd, dec, sp, edge_s, far_s,
    perm, pmat, umat, faces, wt, bt, psib, psie, hots, inv,
    load_sem, out_sem, ce_s, ce_r, fe_s, fe_r, aa_s, aa_r, fx_s, fx_r, cd_s, cd_r, fd_s, fd_r, st_s, st_r,
):
    s, h = lax.axis_index("space"), lax.axis_index("chan")
    count = lax.axis_size("space")
    pos = s % WINDOW
    base = s - pos
    other = (s, 1 - h)
    after, before = s + 1, s - 1
    has_before, has_after = s > 0, s < count - 1
    has_near = jnp.where(h == 0, s, count - 1 - s) > 0
    ch = pl.ds(pl.multiple_of(16 * h, 16), 16)

    def send(src, dst, ssem, rsem, device):
        return pltpu.make_async_remote_copy(
            src_ref=src, dst_ref=dst, send_sem=ssem, recv_sem=rsem,
            device_id=device, device_id_type=pl.DeviceIdType.MESH,
        )

    load_f = pltpu.make_async_copy(feat, fv, load_sem.at[0])
    load_c = pltpu.make_async_copy(cfield, cv, load_sem.at[1])
    load_p = pltpu.make_async_copy(perm_h, perm, load_sem.at[15])
    load_q = pltpu.make_async_copy(face_h, faces, load_sem.at[16])
    for copy in (load_f, load_p, load_q, load_c):
        copy.start()
    ends = (
        (nb_h, nb_s), (oct_h, oct_s), (own_h, own_s), (nb_h, nb_v), (ew_h, ew), (eb_h, eb),
        (cw_h, cw), (cb_h, cb), (dw_h, dw), (db_h, db), (psi_h, psi), (pmat_h, pmat), (umat_h, umat),
    )
    small = [pltpu.make_async_copy(a, b, load_sem.at[2 + n]) for n, (a, b) in enumerate(ends)]
    for copy in small:
        copy.start()

    barrier = pltpu.get_barrier_semaphore()
    peers = [(base + (pos + o) % WINDOW, h) for o in range(1, WINDOW)]
    def greet(device):
        pl.semaphore_signal(barrier, inc=1, device_id=device, device_id_type=pl.DeviceIdType.MESH)

    for device in peers + [other]:
        greet(device)

    @pl.when(has_before)
    def _():
        greet((before, 0))
        greet((before, 1))

    @pl.when(has_after)
    def _():
        greet((after, 0))
        greet((after, 1))

    def pack(rows, which, out):
        width = rows.shape[1]
        got = dot(rows.reshape(8 * width, 512), faces[which]).astype(BF).reshape(8, width, 256)
        out[0:8] = got[:, :, :128]
        for b in range(4):
            lane = iota((width, 128), 1)
            out[8 + b] = jnp.where(lane < 64, got[b, :, 128:], pltpu.roll(got[4 + b, :, 128:], 64, 1))

    def unpack(got, which, pool):
        right = [got[8 + b] for b in range(4)]
        right = right + [pltpu.roll(x, 64, 1) for x in right]
        wide = jnp.concatenate([got[0:8].reshape(256, 128), jnp.concatenate(right, axis=0)], axis=1)
        full = lax.dot_general(wide, faces[which], NT, preferred_element_type=F32)
        pool[near, :, :] = full.astype(BF).reshape(8, 32, 512)

    inner, edge = 8 * (1 - h), 8 * h
    near = pl.ds(32 + 24 * (1 - h), 8)

    load_f.wait()
    load_p.wait()
    for g in range(2):
        part = fv[:, 16 * g : 16 * g + 16, :].reshape(256, 512)
        pool_e[16 * g : 16 * g + 16, ch, :] = dot(perm[...], part).astype(BF).reshape(16, 16, 512)
    load_q.wait()
    pack(pool_e[24:32, ch, :], 1, pe.at[1])
    pack(pool_e[0:8, ch, :], 0, pe.at[0])
    load_c.wait()
    for g in range(2):
        part = cv[:, 16 * g : 16 * g + 16, :].reshape(256, 512)
        ct[16 * g : 16 * g + 16] = dot(perm[...], part).astype(BF).reshape(16, 16, 512)
    extra = jnp.where(has_before, 2, 0) + jnp.where(has_after, 2, 0)
    pl.semaphore_wait(barrier, WINDOW + extra)

    face_up = send(pe.at[1], qe.at[:, ch], fe_s.at[0], fe_r.at[h], (after, 0))
    face_down = send(pe.at[0], qe.at[:, ch], fe_s.at[1], fe_r.at[h], (before, 1))
    both = send(pool_e.at[0:32, ch], pool_e.at[0:32, ch], ce_s, ce_r, other)
    pl.when(has_after)(face_up.start)
    pl.when(has_before)(face_down.start)
    spread_out = []
    for o in range(1, WINDOW):
        to = (pos + o) % WINDOW
        copy = send(
            ct.at[pl.ds(2 * to, 2)], fr.at[pl.ds(2 * pos, 2)], aa_s.at[o], aa_r.at[o], (base + to, h)
        )
        copy.start()
        spread_out.append(copy)
    both.start()
    fr[pl.ds(2 * pos, 2)] = ct[pl.ds(2 * pos, 2)]

    for copy in small:
        copy.wait()
    eye = (iota((32, 32), 0) == iota((32, 32), 1)).astype(BF)
    for n, (w, b) in enumerate(((ew, eb), (cw, cb), (dw, db))):
        flat = w[...].reshape(224, 32)
        wt[n] = lax.dot_general(eye, flat, NT, preferred_element_type=F32).astype(BF)
        spread = jnp.where(iota((32, 32), 0) == iota((32, 32), 1), b[...], 0.0)
        bt[n] = jnp.broadcast_to(jnp.sum(spread, axis=1, keepdims=True), (32, 128))
    tile = (iota((32, 512), 0) == (iota((32, 512), 1) & 31)).astype(BF)
    wide = dot(psi[...], tile)
    for out, width, used in ((psib, 16, 48), (psie, 8, 24)):
        size = out.shape
        pick = [jnp.broadcast_to(wide[m : m + 1, : size[1]], (width, size[1])) for m in range(3)]
        if used < size[0]:
            pick.append(jnp.zeros((size[0] - used, size[1]), F32))
        same = (iota(size, 0) & (width - 1)) == (iota(size, 1) >> 5)
        out[...] = jnp.where(same, jnp.concatenate(pick, axis=0), 0.0).astype(BF)
    pool_e[ABSENT] = jnp.zeros((32, 512), BF)
    pool_d[ABSENT] = jnp.zeros((32, 512), BF)
    at = nb_v[...]
    rel = jnp.where(at < 0, -1, at - 32 * s + 8).astype(F32).astype(BF)
    rel = lax.dot_general(eye, rel, NT, preferred_element_type=F32)
    place = iota((32, 48), 1).astype(F32)
    for d in range(6):
        hots[d] = (place == rel[:, d : d + 1]).astype(BF)
    for kl in range(2):
        for o in range(8):
            found = jnp.int32(0)
            for child in range(8):
                hit = oct_s[16 * h + 8 * kl + child] == o
                found = jnp.where(hit, jnp.int32(8 * kl + child), found)
            inv[8 * kl + o] = found

    def fine(pool, n, out, first):
        weight, bias = wt[n], bt[n][:, :1]

        def body(t, carry):
            local = first + t
            row = 16 * h + local

            def spot(d):
                at = nb_s[d, row]
                rel = at - 32 * s
                return jnp.where(at < 0, ABSENT, rel & 63)

            spots = [spot(d) for d in range(6)]
            nb = lambda d, q: pool[spots[d], :, 128 * q : 128 * q + 128]
            out[local] = conv(quarters(pool[row]), nb, weight, bias)
            return carry

        lax.fori_loop(0, 8, body, 0)

    def pool_half(first):
        rows = enc[pl.ds(first, 8)].reshape(256, 512)
        pooled[pl.ds(first, 8)] = dot(rows, pmat[...]).astype(BF).reshape(8, 32, 256)

    both.wait_recv()
    fine(pool_e, 0, enc, inner)
    pool_half(inner)
    @pl.when(has_near)
    def _():
        for c in range(2):
            chc = pl.ds(16 * c, 16)
            send(pe.at[0], qe.at[:, chc], fe_s.at[0], fe_r.at[c], (s, 1 - h)).wait_recv()
        unpack(qe, 1 - h, pool_e)

    fine(pool_e, 0, enc, edge)
    pool_half(edge)

    for copy in spread_out:
        copy.wait_recv()
    ow = [own_s[0, n] for n in range(4)]
    slot = []
    for n in range(4):
        rank = jnp.int32(0)
        for m in range(n):
            rank = rank + jnp.where(ow[m] == ow[n], 1, 0)
        slot.append(2 * ow[n] + rank)
    for kl in range(2):
        mine = jnp.where(h == 0, slot[kl], slot[2 + kl])
        theirs = jnp.where(h == 0, slot[2 + kl], slot[kl])
        fsend[kl] = fr[theirs]
        fsel[kl, ch, :] = fr[mine]
    swap = send(fsend, fsel.at[:, ch], fx_s, fx_r, other)
    swap.start()

    def gather(kl):
        acc = [None, None]
        for o in range(8):
            part = pooled[inv[8 * kl + o]]
            step = 32 * ((o >> 1) & 1) + 4 * (o & 1)
            part = pltpu.roll(part, step, 1) if step else part
            acc[o >> 2] = part if acc[o >> 2] is None else acc[o >> 2] + part
        return jnp.concatenate(acc, axis=1)

    gathered = [gather(h), gather(1 - h)]
    swap.wait_recv()
    nothing = jnp.zeros((32, 128), BF)

    def coarse(kl, children):
        cin = (children.astype(F32) + fsel[kl].astype(F32)).astype(BF)
        cout = conv(quarters(cin), lambda d, q: nothing, wt[1], bt[1][:, :1])
        parts = []
        for o in range(8):
            part = cout[:, 256 * (o >> 2) : 256 * (o >> 2) + 256]
            step = 32 * ((o >> 1) & 1) + 4 * (o & 1)
            parts.append(pltpu.roll(part, 256 - step, 1) if step else part)
        up = dot(jnp.concatenate(parts, axis=0), umat[...])
        eup[pl.ds(8 * kl, 8)] = up.astype(BF).reshape(8, 32, 512)

    def decoder_in(first):
        def body(t, carry):
            local = first + t
            row = 16 * h + local
            up = eup[first + oct_s[row]]
            pool_d[row] = (enc[local].astype(F32) + up.astype(F32)).astype(BF)
            return carry

        lax.fori_loop(0, 8, body, 0)

    partner = (s + 2 * h - 1, 1 - h)
    coarse(h, gathered[0])
    decoder_in(edge)
    edge_rows = pl.ds(16 * h + edge, 8)
    pack(pool_d[edge_rows], h, pd)
    face_d = send(pd, qd, fd_s, fd_r, partner)
    pl.when(has_near)(face_d.start)
    cross = [send(pool_d.at[edge_rows], pool_d.at[edge_rows], cd_s.at[0], cd_r.at[0], other)]
    cross[0].start()
    coarse(1 - h, gathered[1])
    decoder_in(inner)
    inner_rows = pl.ds(16 * h + inner, 8)
    cross.append(send(pool_d.at[inner_rows], pool_d.at[inner_rows], cd_s.at[1], cd_r.at[1], other))
    cross[1].start()
    cross[0].wait_recv()
    cross[1].wait_recv()
    fine(pool_d, 2, dec, inner)

    @pl.when(has_near)
    def _():
        face_d.wait_recv()
        unpack(qd, 1 - h, pool_d)

    fine(pool_d, 2, dec, edge)

    edge_s[...] = dot(psie[...], dec[pl.ds(edge, 8)].reshape(256, 512)).astype(BF)
    side = s + 2 * h - 1
    far = [send(edge_s, far_s.at[1 - h], st_s.at[1 + c], st_r.at[2 - h], (side, c)) for c in range(2)]
    for copy in far:
        pl.when(has_near)(copy.start)
    own_rows = pl.ds(pl.multiple_of(16 * h, 16), 16)
    sp[:, own_rows, :] = dot(psib[...], dec[...].reshape(512, 512)).astype(BF).reshape(3, 16, 512)
    beside = send(sp.at[:, own_rows], sp.at[:, own_rows], st_s.at[0], st_r.at[0], other)
    beside.start()
    beside.wait_recv()
    for n, there in ((0, has_before), (1, has_after)):

        @pl.when(there)
        def _():
            send(edge_s, far_s.at[n], st_s.at[1], st_r.at[1 + n], other).wait_recv()

        @pl.when(jnp.logical_not(there))
        def _():
            far_s[n] = jnp.zeros((32, 512), BF)

    diff = {}
    for m in range(3):
        axes = [a for a in range(3) if a != m]
        hot = jnp.concatenate([hots[2 * a + side_] for a in axes for side_ in range(2)], axis=0)
        mine = sp[m].astype(F32)
        lower, upper = (far_s[n].astype(F32)[8 * m : 8 * m + 8] for n in range(2))
        near_faces = dot(hot, jnp.concatenate([lower, mine, upper], axis=0).astype(BF))
        own = quarters(mine)
        pieces = {2 * a + e: quarters(near_faces[64 * n + 32 * e : 64 * n + 32 * e + 32]) for n, a in enumerate(axes) for e in range(2)}
        got = shifts(own, lambda d, q: pieces[d][q] if d in pieces else own[q])
        for a in axes:
            diff[a, m] = [0.5 * (x - y) for x, y in zip(got[2 * a + 1], got[2 * a])]
    for m in range(3):
        a, b = (m + 1) % 3, (m + 2) % 3
        vel[m] = jnp.concatenate([x - y for x, y in zip(diff[a, b], diff[b, a])], axis=1)
    store = pltpu.make_async_copy(vel, vel_h, out_sem)
    store.start()

    pl.when(has_after)(face_up.wait_send)
    pl.when(has_before)(face_down.wait_send)
    for copy in spread_out + cross + [both, swap, beside]:
        copy.wait_send()
    for copy in [face_d] + far:
        pl.when(has_near)(copy.wait_send)
    store.wait()


def on_device(features, neighbours, octants, owners, coarse_field, ew, eb, cw, cb, dw, db, psi):
    hbm = pl.BlockSpec(memory_space=pltpu.HBM)
    dma = pltpu.SemaphoreType.DMA
    v = lambda *shape: pltpu.VMEM(shape, BF)
    f = lambda *shape: pltpu.VMEM(shape, F32)
    return pl.pallas_call(
        kernel,
        out_shape=jax.ShapeDtypeStruct((3, 32, 512), F32),
        in_specs=[hbm] * 16,
        out_specs=hbm,
        scratch_shapes=[
            pltpu.SMEM((6, 32), jnp.int32), pltpu.SMEM((32,), jnp.int32), pltpu.SMEM((1, 4), jnp.int32),
            pltpu.VMEM((6, 32), jnp.int32), v(7, 32, 32), f(1, 32), v(7, 32, 32), f(1, 32),
            v(7, 32, 32), f(1, 32), v(3, 32), f(3, 32, 512),
            v(16, 32, 512), v(16, 32, 512), v(64, 32, 512), v(2, 12, 16, 128), v(12, 32, 128),
            v(32, 16, 512), v(32, 16, 512), v(2, 32, 512), v(2, 16, 512),
            v(16, 32, 512), v(16, 32, 256), v(16, 32, 512), v(64, 32, 512), v(12, 32, 128), v(12, 32, 128),
            v(16, 32, 512), v(3, 32, 512), v(32, 512), v(2, 32, 512),
            v(256, 256), v(512, 256), v(256, 512), v(2, 512, 256), v(3, 32, 224), pltpu.VMEM((3, 32, 128), F32),
            v(48, 512), v(32, 256), v(6, 32, 48), pltpu.SMEM((16,), jnp.int32),
            dma((17,)), dma, dma, dma, dma((2,)), dma((2,)), dma((16,)), dma((16,)), dma, dma,
            dma((2,)), dma((2,)), dma, dma, dma((3,)), dma((3,)),
        ],
        compiler_params=pltpu.CompilerParams(
            collective_id=0, has_side_effects=True, vmem_limit_bytes=63 * 1024 * 1024
        ),
    )(
        features, coarse_field, neighbours.T, octants, owners.reshape(1, 4),
        ew, eb.reshape(1, 32), cw, cb.reshape(1, 32), dw, db.reshape(1, 32), psi.T, *tables(),
    )


def solution(mesh):
    split, rows = P("chan", "space", None), P("space", None)
    return jax.shard_map(
        on_device,
        mesh=mesh,
        in_specs=(split, rows, P("space"), rows, split) + (P(),) * 7,
        out_specs=P(None, "space", None),
        check_vma=False,
    )
```

time: 51.9 us -> 39.6 us (0.76)
  the two profiles are of different devices: /device:TPU:1 before, /device:TPU:25 now
where the time goes in v2:
time: 39.6 us; the launch traced here: 39.5 us
  Pallas kernels  37.9 us (96%)
  local copies, waits for them, and re-layouts  1.62 us (4%)
    pallas_call x1, Pallas kernels, on_device(): pl.pallas_call(kernel, out_shape=jax.ShapeDtypeStruct((3, 32, 512), F32),...  37.9 us
    unnamed x1, local copies, waits for them, and re-layouts  1.62 us

profile of v2, /device:TPU:25, one launch (start us, length us, event | category | flops | bytes accessed | tf_op | source)
XLA Modules:
  0.0 39.5 jit_solution(18355756247229486942)
XLA Ops:
  0.0 37.9 %shard_map.154 = f32[3,32,512]{2,1,0:T(8,128)} custom-call(bf16[16,32,512]{2,1,0:T(8,128)(2,1)} %feat.1, bf16[16,32,512]{2,1,0:T(8,128)(2,1)} %cfield.1, s32[6,32]{1,0:T(8,128)} %bitcast.6, s32[32]{0:T(128)} %oct_h.1, s32[1,4]{1,0:T(1,128)} %bitcast.8, bf16[7,32,32]{2,1,0:T(8,128)(2,1)} %ew_h.1, f32[1,32]{1,0:T(1,128)} %bitcast.9, bf16[7,32,32]{2,1,0:T(8,128)(2,1)} %cw_h.1, ...), custom_call_target="tpu_custom_call" | custom-call | tf_op jit(solution)/shard_map/pallas_call | solution.py:372
  37.9 1.6 %copy.18 = f32[3,32,512]{2,1,0:T(8,128)} copy(f32[3,32,512]{2,1,0:T(8,128)} %shard_map.154) | data formatting | bytes 393216

commit v3 on v2

--- a/solution.py
+++ b/solution.py
@@ -91,12 +91,49 @@
             device_id=device, device_id_type=pl.DeviceIdType.MESH,
         )
 
+    barrier = pltpu.get_barrier_semaphore()
+    peers = [(base + (pos + o) % WINDOW, h) for o in range(1, WINDOW)]
+    def greet(device):
+        pl.semaphore_signal(barrier, inc=1, device_id=device, device_id_type=pl.DeviceIdType.MESH)
+
+    for device in peers + [other]:
+        greet(device)
+
+    @pl.when(has_before)
+    def _():
+        greet((before, 0))
+        greet((before, 1))
+
+    @pl.when(has_after)
+    def _():
+        greet((after, 0))
+        greet((after, 1))
+
     load_f = pltpu.make_async_copy(feat, fv, load_sem.at[0])
     load_c = pltpu.make_async_copy(cfield, cv, load_sem.at[1])
     load_p = pltpu.make_async_copy(perm_h, perm, load_sem.at[15])
     load_q = pltpu.make_async_copy(face_h, faces, load_sem.at[16])
     for copy in (load_f, load_p, load_q, load_c):
         copy.start()
+
+    def pack(rows, which, out):
+        width = rows.shape[1]
+        got = dot(rows.reshape(8 * width, 512), faces[which]).astype(BF).reshape(8, width, 256)
+        out[0:8] = got[:, :, :128]
+        for b in range(4):
+            lane = iota((width, 128), 1)
+            out[8 + b] = jnp.where(lane < 64, got[b, :, 128:], pltpu.roll(got[4 + b, :, 128:], 64, 1))
+
+    def unpack(got, which, pool):
+        right = [got[8 + b] for b in range(4)]
+        right = right + [pltpu.roll(x, 64, 1) for x in right]
+        wide = jnp.concatenate([got[0:8].reshape(256, 128), jnp.concatenate(right, axis=0)], axis=1)
+        full = lax.dot_general(wide, faces[which], NT, preferred_element_type=F32)
+        pool[near, :, :] = full.astype(BF).reshape(8, 32, 512)
+
+    inner, edge = 8 * (1 - h), 8 * h
+    near = pl.ds(32 + 24 * (1 - h), 8)
+
     ends = (
         (nb_h, nb_s), (oct_h, oct_s), (own_h, own_s), (nb_h, nb_v), (ew_h, ew), (eb_h, eb),
         (cw_h, cw), (cb_h, cb), (dw_h, dw), (db_h, db), (psi_h, psi), (pmat_h, pmat), (umat_h, umat),
@@ -104,43 +141,6 @@
     small = [pltpu.make_async_copy(a, b, load_sem.at[2 + n]) for n, (a, b) in enumerate(ends)]
     for copy in small:
         copy.start()
-
-    barrier = pltpu.get_barrier_semaphore()
-    peers = [(base + (pos + o) % WINDOW, h) for o in range(1, WINDOW)]
-    def greet(device):
-        pl.semaphore_signal(barrier, inc=1, device_id=device, device_id_type=pl.DeviceIdType.MESH)
-
-    for device in peers + [other]:
-        greet(device)
-
-    @pl.when(has_before)
-    def _():
-        greet((before, 0))
-        greet((before, 1))
-
-    @pl.when(has_after)
-    def _():
-        greet((after, 0))
-        greet((after, 1))
-
-    def pack(rows, which, out):
-        width = rows.shape[1]
-        got = dot(rows.reshape(8 * width, 512), faces[which]).astype(BF).reshape(8, width, 256)
-        out[0:8] = got[:, :, :128]
-        for b in range(4):
-            lane = iota((width, 128), 1)
-            out[8 + b] = jnp.where(lane < 64, got[b, :, 128:], pltpu.roll(got[4 + b, :, 128:], 64, 1))
-
-    def unpack(got, which, pool):
-        right = [got[8 + b] for b in range(4)]
-        right = right + [pltpu.roll(x, 64, 1) for x in right]
-        wide = jnp.concatenate([got[0:8].reshape(256, 128), jnp.concatenate(right, axis=0)], axis=1)
-        full = lax.dot_general(wide, faces[which], NT, preferred_element_type=F32)
-        pool[near, :, :] = full.astype(BF).reshape(8, 32, 512)
-
-    inner, edge = 8 * (1 - h), 8 * h
-    near = pl.ds(32 + 24 * (1 - h), 8)
-
     load_f.wait()
     load_p.wait()
     for g in range(2):
@@ -162,7 +162,7 @@
     pl.when(has_after)(face_up.start)
     pl.when(has_before)(face_down.start)
     spread_out = []
-    for o in range(1, WINDOW):
+    for o in (1, 7, 8, 9, 15, 2, 6, 10, 14, 3, 5, 11, 13, 4, 12):
         to = (pos + o) % WINDOW
         copy = send(
             ct.at[pl.ds(2 * to, 2)], fr.at[pl.ds(2 * pos, 2)], aa_s.at[o], aa_r.at[o], (base + to, h)
@@ -222,7 +222,7 @@
             out[local] = conv(quarters(pool[row]), nb, weight, bias)
             return carry
 
-        lax.fori_loop(0, 8, body, 0)
+        lax.fori_loop(0, 8, body, 0, unroll=8)
 
     def pool_half(first):
         rows = enc[pl.ds(first, 8)].reshape(256, 512)
@@ -290,7 +290,7 @@
             pool_d[row] = (enc[local].astype(F32) + up.astype(F32)).astype(BF)
             return carry
 
-        lax.fori_loop(0, 8, body, 0)
+        lax.fori_loop(0, 8, body, 0, unroll=8)
 
     partner = (s + 2 * h - 1, 1 - h)
     coarse(h, gathered[0])

time: 39.6 us -> 37 us (0.934)
  Pallas kernels: 37.9 us -> 35.3 us
    pallas_call x1, Pallas kernels: 37.9 us -> 35.3 us  [on_device(): pl.pallas_call(kernel, out_shape=jax.ShapeDtypeStruct((3, 32, 512), F32),...]
where the time goes in v3:
time: 37 us; the launch traced here: 36.9 us
  Pallas kernels  35.3 us (95%)
  local copies, waits for them, and re-layouts  1.62 us (4%)
    pallas_call x1, Pallas kernels, on_device(): pl.pallas_call(kernel, out_shape=jax.ShapeDtypeStruct((3, 32, 512), F32),...  35.3 us
    unnamed x1, local copies, waits for them, and re-layouts  1.62 us

profile of v3, /device:TPU:25, one launch (start us, length us, event | category | flops | bytes accessed | tf_op | source)
XLA Modules:
  0.0 36.9 jit_solution(15875462476122538236)
XLA Ops:
  0.0 35.3 %shard_map.154 = f32[3,32,512]{2,1,0:T(8,128)} custom-call(bf16[16,32,512]{2,1,0:T(8,128)(2,1)} %feat.1, bf16[16,32,512]{2,1,0:T(8,128)(2,1)} %cfield.1, s32[6,32]{1,0:T(8,128)} %bitcast.6, s32[32]{0:T(128)} %oct_h.1, s32[1,4]{1,0:T(1,128)} %bitcast.8, bf16[7,32,32]{2,1,0:T(8,128)(2,1)} %ew_h.1, f32[1,32]{1,0:T(1,128)} %bitcast.9, bf16[7,32,32]{2,1,0:T(8,128)(2,1)} %cw_h.1, ...), custom_call_target="tpu_custom_call" | custom-call | tf_op jit(solution)/shard_map/pallas_call | solution.py:372
  35.3 1.6 %copy.18 = f32[3,32,512]{2,1,0:T(8,128)} copy(f32[3,32,512]{2,1,0:T(8,128)} %shard_map.154) | data formatting | bytes 393216

commit v4 on v3

--- a/solution.py
+++ b/solution.py
@@ -72,7 +72,7 @@
     perm_h, pmat_h, umat_h, face_h,
     vel_h,
     nb_s, oct_s, own_s, nb_v, ew, eb, cw, cb, dw, db, psi, vel, fv, cv, pool_e, pe, qe, ct, fr, fsel, fsend, enc, pooled, eup, pool_d, pd, qd, dec, sp, edge_s, far_s,
-    perm, pmat, umat, faces, wt, bt, psib, psie, hots, inv,
+    perm, pmat, umat, faces, wt, bt, psib, psie, hots, inv, enc_p, up_p, uface,
     load_sem, out_sem, ce_s, ce_r, fe_s, fe_r, aa_s, aa_r, fx_s, fx_r, cd_s, cd_r, fd_s, fd_r, st_s, st_r,
 ):
     s, h = lax.axis_index("space"), lax.axis_index("chan")
@@ -96,7 +96,7 @@
     def greet(device):
         pl.semaphore_signal(barrier, inc=1, device_id=device, device_id_type=pl.DeviceIdType.MESH)
 
-    for device in peers + [other]:
+    for device in [peers[o - 1] for o in (4, 12, 3, 5, 11, 13, 2, 6, 10, 14, 1, 7, 9, 15, 8)] + [other]:
         greet(device)
 
     @pl.when(has_before)
@@ -159,8 +159,6 @@
     face_up = send(pe.at[1], qe.at[:, ch], fe_s.at[0], fe_r.at[h], (after, 0))
     face_down = send(pe.at[0], qe.at[:, ch], fe_s.at[1], fe_r.at[h], (before, 1))
     both = send(pool_e.at[0:32, ch], pool_e.at[0:32, ch], ce_s, ce_r, other)
-    pl.when(has_after)(face_up.start)
-    pl.when(has_before)(face_down.start)
     spread_out = []
     for o in (1, 7, 8, 9, 15, 2, 6, 10, 14, 3, 5, 11, 13, 4, 12):
         to = (pos + o) % WINDOW
@@ -169,6 +167,9 @@
         )
         copy.start()
         spread_out.append(copy)
+        if o == 6:
+            pl.when(has_after)(face_up.start)
+            pl.when(has_before)(face_down.start)
     both.start()
     fr[pl.ds(2 * pos, 2)] = ct[pl.ds(2 * pos, 2)]
 
@@ -180,6 +181,7 @@
         wt[n] = lax.dot_general(eye, flat, NT, preferred_element_type=F32).astype(BF)
         spread = jnp.where(iota((32, 32), 0) == iota((32, 32), 1), b[...], 0.0)
         bt[n] = jnp.broadcast_to(jnp.sum(spread, axis=1, keepdims=True), (32, 128))
+    uface[...] = dot(umat[...], faces[h]).astype(BF)
     tile = (iota((32, 512), 0) == (iota((32, 512), 1) & 31)).astype(BF)
     wide = dot(psi[...], tile)
     for out, width, used in ((psib, 16, 48), (psie, 8, 24)):
@@ -240,6 +242,7 @@
 
     fine(pool_e, 0, enc, edge)
     pool_half(edge)
+    enc_p[...] = dot(enc[pl.ds(edge, 8)].reshape(256, 512), faces[h]).astype(BF).reshape(8, 32, 256)
 
     for copy in spread_out:
         copy.wait_recv()
@@ -279,7 +282,10 @@
             part = cout[:, 256 * (o >> 2) : 256 * (o >> 2) + 256]
             step = 32 * ((o >> 1) & 1) + 4 * (o & 1)
             parts.append(pltpu.roll(part, 256 - step, 1) if step else part)
-        up = dot(jnp.concatenate(parts, axis=0), umat[...])
+        return jnp.concatenate(parts, axis=0)
+
+    def spread_up(kl, parts):
+        up = dot(parts, umat[...])
         eup[pl.ds(8 * kl, 8)] = up.astype(BF).reshape(8, 32, 512)
 
     def decoder_in(first):
@@ -293,15 +299,24 @@
         lax.fori_loop(0, 8, body, 0, unroll=8)
 
     partner = (s + 2 * h - 1, 1 - h)
-    coarse(h, gathered[0])
+    parts = coarse(h, gathered[0])
+    up_p[...] = dot(parts, uface[...]).astype(BF).reshape(8, 32, 256)
+    sums = []
+    for t in range(8):
+        up = up_p[oct_s[16 * h + edge + t]]
+        sums.append((enc_p[t].astype(F32) + up.astype(F32)).astype(BF))
+        pd[t] = sums[t][:, :128]
+    for b in range(4):
+        lane = iota((32, 128), 1)
+        pd[8 + b] = jnp.where(lane < 64, sums[b][:, 128:], pltpu.roll(sums[4 + b][:, 128:], 64, 1))
+    face_d = send(pd, qd, fd_s, fd_r, partner)
+    pl.when(has_near)(face_d.start)
+    spread_up(h, parts)
     decoder_in(edge)
     edge_rows = pl.ds(16 * h + edge, 8)
-    pack(pool_d[edge_rows], h, pd)
-    face_d = send(pd, qd, fd_s, fd_r, partner)
-    pl.when(has_near)(face_d.start)
     cross = [send(pool_d.at[edge_rows], pool_d.at[edge_rows], cd_s.at[0], cd_r.at[0], other)]
     cross[0].start()
-    coarse(1 - h, gathered[1])
+    spread_up(1 - h, coarse(1 - h, gathered[1]))
     decoder_in(inner)
     inner_rows = pl.ds(16 * h + inner, 8)
     cross.append(send(pool_d.at[inner_rows], pool_d.at[inner_rows], cd_s.at[1], cd_r.at[1], other))
@@ -337,7 +352,7 @@
         def _():
             far_s[n] = jnp.zeros((32, 512), BF)
 
-    diff = {}
+    diff, stores = {}, []
     for m in range(3):
         axes = [a for a in range(3) if a != m]
         hot = jnp.concatenate([hots[2 * a + side_] for a in axes for side_ in range(2)], axis=0)
@@ -352,8 +367,8 @@
     for m in range(3):
         a, b = (m + 1) % 3, (m + 2) % 3
         vel[m] = jnp.concatenate([x - y for x, y in zip(diff[a, b], diff[b, a])], axis=1)
-    store = pltpu.make_async_copy(vel, vel_h, out_sem)
-    store.start()
+        stores.append(pltpu.make_async_copy(vel.at[m], vel_h.at[m], out_sem.at[m]))
+        stores[m].start()
 
     pl.when(has_after)(face_up.wait_send)
     pl.when(has_before)(face_down.wait_send)
@@ -361,7 +376,8 @@
         copy.wait_send()
     for copy in [face_d] + far:
         pl.when(has_near)(copy.wait_send)
-    store.wait()
+    for copy in stores:
+        copy.wait()
 
 
 def on_device(features, neighbours, octants, owners, coarse_field, ew, eb, cw, cb, dw, db, psi):
@@ -383,8 +399,8 @@
             v(16, 32, 512), v(16, 32, 256), v(16, 32, 512), v(64, 32, 512), v(12, 32, 128), v(12, 32, 128),
             v(16, 32, 512), v(3, 32, 512), v(32, 512), v(2, 32, 512),
             v(256, 256), v(512, 256), v(256, 512), v(2, 512, 256), v(3, 32, 224), pltpu.VMEM((3, 32, 128), F32),
-            v(48, 512), v(32, 256), v(6, 32, 48), pltpu.SMEM((16,), jnp.int32),
-            dma((17,)), dma, dma, dma, dma((2,)), dma((2,)), dma((16,)), dma((16,)), dma, dma,
+            v(48, 512), v(32, 256), v(6, 32, 48), pltpu.SMEM((16,), jnp.int32), v(8, 32, 256), v(8, 32, 256), v(256, 256),
+            dma((17,)), dma((3,)), dma, dma, dma((2,)), dma((2,)), dma((16,)), dma((16,)), dma, dma,
             dma((2,)), dma((2,)), dma, dma, dma((3,)), dma((3,)),
         ],
         compiler_params=pltpu.CompilerParams(

time: 37 us -> 36.6 us (0.989)
  Pallas kernels: 35.3 us -> 34.9 us
    pallas_call x1, Pallas kernels: 35.3 us -> 34.9 us  [on_device(): pl.pallas_call(kernel, out_shape=jax.ShapeDtypeStruct((3, 32, 512), F32),...]
where the time goes in v4:
time: 36.6 us; the launch traced here: 36.5 us
  Pallas kernels  34.9 us (95%)
  local copies, waits for them, and re-layouts  1.62 us (4%)
    pallas_call x1, Pallas kernels, on_device(): pl.pallas_call(kernel, out_shape=jax.ShapeDtypeStruct((3, 32, 512), F32),...  34.9 us
    unnamed x1, local copies, waits for them, and re-layouts  1.62 us

profile of v4, /device:TPU:25, one launch (start us, length us, event | category | flops | bytes accessed | tf_op | source)
XLA Modules:
  0.0 36.5 jit_solution(10234813910465330558)
XLA Ops:
  0.0 34.9 %shard_map.154 = f32[3,32,512]{2,1,0:T(8,128)} custom-call(bf16[16,32,512]{2,1,0:T(8,128)(2,1)} %feat.1, bf16[16,32,512]{2,1,0:T(8,128)(2,1)} %cfield.1, s32[6,32]{1,0:T(8,128)} %bitcast.6, s32[32]{0:T(128)} %oct_h.1, s32[1,4]{1,0:T(1,128)} %bitcast.8, bf16[7,32,32]{2,1,0:T(8,128)(2,1)} %ew_h.1, f32[1,32]{1,0:T(1,128)} %bitcast.9, bf16[7,32,32]{2,1,0:T(8,128)(2,1)} %cw_h.1, ...), custom_call_target="tpu_custom_call" | custom-call | tf_op jit(solution)/shard_map/pallas_call | solution.py:388
  34.9 1.6 %copy.18 = f32[3,32,512]{2,1,0:T(8,128)} copy(f32[3,32,512]{2,1,0:T(8,128)} %shard_map.154) | data formatting | bytes 393216

commit v5 on v4

--- a/solution.py
+++ b/solution.py
@@ -160,14 +160,14 @@
     face_down = send(pe.at[0], qe.at[:, ch], fe_s.at[1], fe_r.at[h], (before, 1))
     both = send(pool_e.at[0:32, ch], pool_e.at[0:32, ch], ce_s, ce_r, other)
     spread_out = []
-    for o in (1, 7, 8, 9, 15, 2, 6, 10, 14, 3, 5, 11, 13, 4, 12):
+    for o in (1, 7, 9, 15, 2, 6, 10, 14, 3, 5, 11, 13, 4, 12, 8):
         to = (pos + o) % WINDOW
         copy = send(
             ct.at[pl.ds(2 * to, 2)], fr.at[pl.ds(2 * pos, 2)], aa_s.at[o], aa_r.at[o], (base + to, h)
         )
         copy.start()
         spread_out.append(copy)
-        if o == 6:
+        if o == 10:
             pl.when(has_after)(face_up.start)
             pl.when(has_before)(face_down.start)
     both.start()

time: 36.6 us -> 36.6 us (level)
  no operation moved by 1% of the time
where the time goes in v5:
time: 36.6 us; the launch traced here: 36.5 us
  Pallas kernels  34.9 us (95%)
  local copies, waits for them, and re-layouts  1.62 us (4%)
    pallas_call x1, Pallas kernels, on_device(): pl.pallas_call(kernel, out_shape=jax.ShapeDtypeStruct((3, 32, 512), F32),...  34.9 us
    unnamed x1, local copies, waits for them, and re-layouts  1.62 us

profile of v5, /device:TPU:25, one launch (start us, length us, event | category | flops | bytes accessed | tf_op | source)
XLA Modules:
  0.0 36.5 jit_solution(7101038580552505430)
XLA Ops:
  0.0 34.9 %shard_map.154 = f32[3,32,512]{2,1,0:T(8,128)} custom-call(bf16[16,32,512]{2,1,0:T(8,128)(2,1)} %feat.1, bf16[16,32,512]{2,1,0:T(8,128)(2,1)} %cfield.1, s32[6,32]{1,0:T(8,128)} %bitcast.6, s32[32]{0:T(128)} %oct_h.1, s32[1,4]{1,0:T(1,128)} %bitcast.8, bf16[7,32,32]{2,1,0:T(8,128)(2,1)} %ew_h.1, f32[1,32]{1,0:T(1,128)} %bitcast.9, bf16[7,32,32]{2,1,0:T(8,128)(2,1)} %cw_h.1, ...), custom_call_target="tpu_custom_call" | custom-call | tf_op jit(solution)/shard_map/pallas_call | solution.py:388
  34.9 1.6 %copy.18 = f32[3,32,512]{2,1,0:T(8,128)} copy(f32[3,32,512]{2,1,0:T(8,128)} %shard_map.154) | data formatting | bytes 393216
